TPU v7x, 32 devices: a whole 2x2x4 slice. The times are simulated.
32 devices in a mesh: dp: 8 (over z, x), et: 4 (over y, core).
Axes of the slice: x: 2, y: 2, z: 4, core: 2. Of those that a mesh axis runs over, the one named last changes fastest.
Arguments:
- tokens: bfloat16 [1024, 2048], P('dp', 'et'), may hold values from -6 to 6
- cotangent: bfloat16 [1024, 2048], P('dp', 'et'), may hold values from -1.5 to 1.5
- expert_ids: int32 [1024, 8], P('dp'), may hold values from 0 to 15, all different within a row; in each aligned block of 128 rows (0 to 127, 128 to 255, ...) at most 96 rows name the same one
- route_gates: bfloat16 [1024, 8], P('dp'), may hold values from 0.049804688 to 0.3984375
- gate_proj: bfloat16 [16, 2048, 1024], P('dp', None, 'et'), may hold values from -0.125 to 0.125
- up_proj: bfloat16 [16, 2048, 1024], P('dp', None, 'et'), may hold values from -0.125 to 0.125
- down_proj: bfloat16 [16, 1024, 2048], P('dp', 'et'), may hold values from -0.1875 to 0.1875
Outputs:
- mixed: bfloat16 [1024, 2048], P('dp', 'et')
- grad_tokens: bfloat16 [1024, 2048], P('dp', 'et')
- grad_gates: float32 [1024, 8], P('dp')
- grad_gate_proj: float32 [16, 2048, 1024], P('dp', None, 'et')
- grad_up_proj: float32 [16, 2048, 1024], P('dp', None, 'et')
- grad_down_proj: float32 [16, 1024, 2048], P('dp', 'et')
Inputs may be any that keep to these rules, and one draw needn't show every extreme that they name: `expert_ids`: each row names 8 different experts. Among the rows of one device (128 aligned rows), no expert is named more than 96 times, a bound that some block reaches.
All inputs are finite; a program needn't handle non-finite values.
Results may differ from a plain program's by a relative error of at most 0.015.
Values may be sent and summed in bfloat16 or wider, within the bound.
A program may use at most 128 MiB of HBM per device.

v0:
```python
import jax
import jax.numpy as jnp
from jax import lax
from jax.sharding import PartitionSpec as P


def places_in_block(chosen, experts):
    flattened = chosen.reshape(-1)
    onehot = (flattened[:, None] == jnp.arange(experts, dtype=jnp.int32)[None, :]).astype(jnp.int32)
    before = jnp.cumsum(onehot, axis=0) - onehot
    return jnp.sum(before * onehot, axis=1)


def pick_rows(lookup, inputs, cotangent, gate_values, per_token):
    holder = lookup // per_token
    inputs_ext = jnp.concatenate([inputs, jnp.zeros((1, inputs.shape[1]), jnp.bfloat16)], axis=0)
    cotangent_ext = jnp.concatenate(
        [cotangent, jnp.zeros((1, cotangent.shape[1]), jnp.bfloat16)], axis=0
    )
    gates_ext = jnp.concatenate([gate_values, jnp.zeros((1,), jnp.float32)], axis=0)
    picked = inputs_ext[holder]
    scaled = (gates_ext[lookup][:, None] * cotangent_ext[holder].astype(jnp.float32)).astype(
        jnp.bfloat16
    )
    return (picked, scaled)


def local(tokens, cotangent, expert_ids, route_gates, gate_proj, up_proj, down_proj):
    groups = lax.axis_size("dp")
    local_experts = gate_proj.shape[0]
    experts = local_experts * groups
    tok_rows, per_token = expert_ids.shape
    features = gate_proj.shape[1]
    capacity = 3 * tok_rows * per_token // (2 * experts)
    assignments = tok_rows * per_token
    places = places_in_block(expert_ids, experts)
    slot_index = expert_ids.reshape(-1) * capacity + places
    gates_flat = route_gates.reshape(-1).astype(jnp.float32)
    lookup = (
        jnp.full((experts * capacity,), assignments, jnp.int32)
        .at[slot_index]
        .set(jnp.arange(assignments, dtype=jnp.int32))
    )
    full_tokens, full_cot = (
        lax.all_gather(tokens, "et", axis=1, tiled=True),
        lax.all_gather(cotangent, "et", axis=1, tiled=True),
    )
    picked, scaled = pick_rows(lookup, full_tokens, full_cot, gates_flat, per_token)
    expert_in, expert_cot = (
        lax.all_to_all(
            picked.reshape(experts, capacity, features),
            "dp",
            split_axis=0,
            concat_axis=1,
            tiled=True,
        ),
        lax.all_to_all(
            scaled.reshape(experts, capacity, features),
            "dp",
            split_axis=0,
            concat_axis=1,
            tiled=True,
        ),
    )
    pre_gate = jnp.einsum("esd,edf->esf", expert_in, gate_proj, preferred_element_type=jnp.float32)
    pre_up = jnp.einsum("esd,edf->esf", expert_in, up_proj, preferred_element_type=jnp.float32)
    sigmoid_gate = jax.nn.sigmoid(pre_gate)
    silu_gate = pre_gate * sigmoid_gate
    hidden = (silu_gate * pre_up).astype(jnp.bfloat16)
    out_part = jnp.einsum("esf,efd->esd", hidden, down_proj, preferred_element_type=jnp.float32)
    grad_hidden = jnp.einsum(
        "esd,efd->esf", expert_cot, down_proj, preferred_element_type=jnp.float32
    )
    grad_pre_gate = (
        grad_hidden * pre_up * sigmoid_gate * (1.0 + pre_gate * (1.0 - sigmoid_gate))
    ).astype(jnp.bfloat16)
    grad_pre_up = (grad_hidden * silu_gate).astype(jnp.bfloat16)
    grad_down = jnp.einsum("esf,esd->efd", hidden, expert_cot, preferred_element_type=jnp.float32)
    grad_gate_w = jnp.einsum(
        "esd,esf->edf", expert_in, grad_pre_gate, preferred_element_type=jnp.float32
    )
    grad_up_w = jnp.einsum(
        "esd,esf->edf", expert_in, grad_pre_up, preferred_element_type=jnp.float32
    )
    in_part = jnp.einsum(
        "esf,edf->esd", grad_pre_gate, gate_proj, preferred_element_type=jnp.float32
    )
    in_part = in_part + jnp.einsum(
        "esf,edf->esd", grad_pre_up, up_proj, preferred_element_type=jnp.float32
    )
    out_sum, in_sum = (
        lax.psum_scatter(
            out_part.astype(jnp.bfloat16), "et", scatter_dimension=2, tiled=True
        ).astype(jnp.float32),
        lax.psum_scatter(
            in_part.astype(jnp.bfloat16), "et", scatter_dimension=2, tiled=True
        ).astype(jnp.float32),
    )
    back_out, back_grad = (
        lax.all_to_all(out_sum.astype(jnp.bfloat16), "dp", split_axis=1, concat_axis=0, tiled=True),
        lax.all_to_all(in_sum.astype(jnp.bfloat16), "dp", split_axis=1, concat_axis=0, tiled=True),
    )
    slice_width = tokens.shape[1]
    out_rows = (
        back_out.reshape(experts * capacity, slice_width)[slot_index]
        .reshape(tok_rows, per_token, slice_width)
        .astype(jnp.float32)
    )
    grad_rows = (
        back_grad.reshape(experts * capacity, slice_width)[slot_index]
        .reshape(tok_rows, per_token, slice_width)
        .astype(jnp.float32)
    )
    mixed = jnp.sum(route_gates.astype(jnp.float32)[:, :, None] * out_rows, axis=1).astype(
        jnp.bfloat16
    )
    gate_part = jnp.sum(cotangent.astype(jnp.float32)[:, None, :] * out_rows, axis=2)
    grad_gates = lax.psum(gate_part, "et")
    grad_tokens = jnp.sum(grad_rows, axis=1).astype(jnp.bfloat16)
    return (mixed, grad_tokens, grad_gates, grad_gate_w, grad_up_w, grad_down)


def solution(mesh):
    in_specs = (
        P("dp", "et"),
        P("dp", "et"),
        P("dp", None),
        P("dp", None),
        P("dp", None, "et"),
        P("dp", None, "et"),
        P("dp", "et", None),
    )
    out_specs = (
        P("dp", "et"),
        P("dp", "et"),
        P("dp", None),
        P("dp", None, "et"),
        P("dp", None, "et"),
        P("dp", "et", None),
    )
    return jax.shard_map(local, mesh=mesh, in_specs=in_specs, out_specs=out_specs, check_vma=False)
```

profile of v0, /device:TPU:0, one launch (start us, length us, event | category | flops | bytes accessed | tf_op | source)
XLA Modules:
  0.0 543.5 jit_solution(15958044386609027953)
XLA Ops:
  7.2 0.0 copy-start
  7.2 0.8 broadcast_multiply_fusion
  8.0 0.8 copy.37
  8.8 0.1 eq.29
  8.9 0.1 eq.25
  9.0 0.8 copy.44
  9.8 0.1 convert_element_type.70
  9.9 0.1 copy.36
  10.0 0.1 mul.74
  10.1 4.5 reduce-window.6
  14.6 0.1 slice.18
  14.7 0.1 copy.39
  14.9 0.1 copy.40
  14.9 0.1 broadcast_add_fusion
  15.1 4.3 scatter_custom_fusion
  19.5 0.0 copy-start.7
  19.5 8.4 %gather_fusion.2 = f32[1536]{0:T(1024)S(1)} fusion(f32[1025]{0:T(1024)S(1)} %maximum_convert_fusion, s32[2048]{0:T(1024)S(1)} %pad_clamp_fusion), kind=kCustom, calls=%fused_computation.2 | custom fusion | bytes 18432 | tf_op jit(solution)/shard_map/gather | solution.py:22
  27.9 0.1 mul.79
  28.0 8.6 %all_gather.7 = bf16[128,2048]{1,0:T(8,128)(2,1)S(1)} all-gather(bf16[128,512]{1,0:T(8,128)(2,1)S(1)} %copy-done.7), channel_id=1, replica_groups=mesh['dp'=8,'et'=4] {'et'}, dimensions={1}, use_global_device_ids=true | all-gather | bytes 655360 | tf_op jit(solution)/shard_map/all_gather | solution.py:46
  36.7 7.1 %gather_fusion.3 = bf16[1536,2048]{1,0:T(8,128)(2,1)} fusion(bf16[129,2048]{1,0:T(8,128)(2,1)S(1)} %concatenate.15, s32[2048]{0:T(1024)S(1)} %pad_clamp_fusion.1), kind=kCustom, calls=%fused_computation.3 | custom fusion | bytes 12589056 | tf_op jit(solution)/shard_map/gather | solution.py:22
  43.8 6.5 %fusion = bf16[16,96,2048]{2,1,0:T(8,128)(2,1)} fusion(bf16[16,96,2048]{2,1,0:T(8,128)(2,1)} %bitcast.75, f32[16,96]{1,0:T(8,128)S(1)} %mul.79), kind=kLoop, calls=%fused_computation.7 | loop fusion | flops 9437184 | bytes 12589056 | tf_op jit(solution)/shard_map/convert_element_type | solution.py:22
  50.3 5.9 %all-to-all-start.2 = ((bf16[16,96,2048]{2,1,0:T(8,128)(2,1)}), bf16[16,96,2048]{2,1,0:T(8,128)(2,1)}, u32[]{:S(2)}, u32[]{:S(2)}) async-start(bf16[16,96,2048]{2,1,0:T(8,128)(2,1)} %fusion), calls=%async_computation.3 | async-start | bytes 12582912 | tf_op jit(solution)/shard_map/all_to_all | solution.py:57
  56.2 7.0 %all_gather.6 = bf16[128,2048]{1,0:T(8,128)(2,1)S(1)} all-gather(bf16[128,512]{1,0:T(8,128)(2,1)S(1)} %copy-done.8), channel_id=1, replica_groups=mesh['dp'=8,'et'=4] {'et'}, dimensions={1}, use_global_device_ids=true | all-gather | bytes 655360 | tf_op jit(solution)/shard_map/all_gather | solution.py:45
  63.3 7.1 %gather_fusion = bf16[1536,2048]{1,0:T(8,128)(2,1)} fusion(bf16[129,2048]{1,0:T(8,128)(2,1)S(1)} %concatenate.12, s32[2048]{0:T(1024)S(1)} %pad_clamp_fusion.1), kind=kCustom, calls=%fused_computation | custom fusion | bytes 12589056 | tf_op jit(solution)/shard_map/gather | solution.py:21
  70.4 124.6 %all-to-all-done.2 = bf16[16,96,2048]{2,1,0:T(8,128)(2,1)} async-done(((bf16[16,96,2048]{2,1,0:T(8,128)(2,1)}), bf16[16,96,2048]{2,1,0:T(8,128)(2,1)}, u32[]{:S(2)}, u32[]{:S(2)}) %all-to-all-start.2) | async-done | bytes 6291488 | tf_op jit(solution)/shard_map/all_to_all | solution.py:57
  194.9 4.8 all-to-all-start
  199.7 0.2 reduce-scatter.3.cloned.1.call-start
  200.0 6.6 %copy.45 = bf16[2,8,96,2048]{3,2,1,0:T(8,128)(2,1)} copy(bf16[2,8,96,2048]{3,2,0,1:T(8,128)(2,1)} %bitcast.14) | data formatting | bytes 12582912 | tf_op jit(solution)/shard_map/all_to_all | solution.py:57
  206.5 131.0 %all-to-all-done = bf16[16,96,2048]{2,1,0:T(8,128)(2,1)} async-done(((bf16[16,96,2048]{2,1,0:T(8,128)(2,1)}), bf16[16,96,2048]{2,1,0:T(8,128)(2,1)}, u32[]{:S(2)}, u32[]{:S(2)}) %all-to-all-start) | async-done | bytes 6291488 | tf_op jit(solution)/shard_map/all_to_all | solution.py:50
  337.5 3.5 copy.41
  341.1 0.0 copy-start.5
  341.1 1.8 fusion.13
  342.9 1.3 copy-done.1
  344.2 0.0 copy-done.5
  344.2 1.8 fusion.12
  346.1 0.1 slice-done
  346.2 0.7 slice-done.1
  346.9 3.9 multiply_convert_fusion
  350.8 4.4 convolution_convert_fusion
  355.2 0.0 reduce-scatter.3.cloned.1.call-update
  355.2 0.3 reduce-scatter.5.cloned.1.call-start
  355.5 0.0 copy-start.3
  355.5 3.7 fusion.14
  359.2 6.7 %add_convert_fusion = bf16[2,768,2048]{2,1,0:T(8,128)(2,1)} fusion(f32[2,768,2048]{2,1,0:T(8,128)S(1)} %fusion.14, bf16[2,768,256]{2,1,0:T(8,128)(2,1)S(1)} %copy-done.3, bf16[2,2048,256]{2,1,0:T(8,128)(2,1)} %param.12), kind=kOutput, calls=%fused_computation.8 | convolution fusion | flops 1616904192 | bytes 21757952 | tf_op jit(solution)/shard_map/esf,edf->esd/dot_general | solution.py:88
  366.0 0.0 reduce-scatter.5.cloned.1.call-update
  366.0 46.4 %reduce-scatter.3.cloned.1.call-done = bf16[2,768,512]{2,1,0:T(8,128)(2,1)} async-done(((bf16[2,768,2048]{2,1,0:T(8,128)(2,1)}), bf16[2,768,512]{2,1,0:T(8,128)(2,1)}) %reduce-scatter.3.cloned.1.call-update) | async-done | bytes 1572880 | tf_op jit(solution)/shard_map/reduce_scatter | solution.py:92
  412.4 4.2 copy.42
  416.5 5.5 %all-to-all-start.1 = ((bf16[2,768,512]{2,0,1:T(2,128)(2,1)}), bf16[2,768,512]{2,0,1:T(2,128)(2,1)}, u32[]{:S(2)}, u32[]{:S(2)}) async-start(bf16[2,768,512]{2,0,1:T(2,128)(2,1)} %copy.42), calls=%async_computation.2 | async-start | bytes 3145728 | tf_op jit(solution)/shard_map/all_to_all | solution.py:100
  422.0 51.4 %reduce-scatter.5.cloned.1.call-done = bf16[2,768,512]{2,1,0:T(8,128)(2,1)} async-done(((bf16[2,768,2048]{2,1,0:T(8,128)(2,1)}), bf16[2,768,512]{2,1,0:T(8,128)(2,1)}) %reduce-scatter.5.cloned.1.call-update) | async-done | bytes 1572880 | tf_op jit(solution)/shard_map/reduce_scatter | solution.py:95
  473.5 4.2 copy.46
  477.6 5.7 %all-to-all-start.3 = ((bf16[2,768,512]{2,0,1:T(2,128)(2,1)}), bf16[2,768,512]{2,0,1:T(2,128)(2,1)}, u32[]{:S(2)}, u32[]{:S(2)}) async-start(bf16[2,768,512]{2,0,1:T(2,128)(2,1)} %copy.46), calls=%async_computation.5 | async-start | bytes 3145728 | tf_op jit(solution)/shard_map/all_to_all | solution.py:101
  483.3 0.1 copy.35
  483.5 0.0 copy-start.4
  483.5 6.7 %fusion.17 = f32[2,256,2048]{2,1,0:T(8,128)} fusion(bf16[2,768,256]{2,1,0:T(8,128)(2,1)S(1)} %get-tuple-element.16, bf16[2,768,2048]{2,1,0:T(8,128)(2,1)} %bitcast.70), kind=kOutput, calls=%fused_computation.50 | convolution fusion | flops 1610612736 | bytes 11272192 | tf_op jit(solution)/shard_map/esf,esd->efd/dot_general | solution.py:78
  490.2 7.4 %fusion.16 = f32[2,2048,256]{2,1,0:T(8,128)} fusion(bf16[2,768,2048]{2,1,0:T(8,128)(2,1)} %bitcast.68, bf16[2,768,256]{2,1,0:T(8,128)(2,1)S(1)} %copy-done.4), kind=kOutput, calls=%fused_computation.49 | convolution fusion | flops 1610612736 | bytes 11272192 | tf_op jit(solution)/shard_map/esd,esf->edf/dot_general | solution.py:82
  497.6 7.4 %fusion.15 = f32[2,2048,256]{2,1,0:T(8,128)} fusion(bf16[2,768,2048]{2,1,0:T(8,128)(2,1)} %bitcast.69, bf16[2,768,256]{2,1,0:T(8,128)(2,1)S(1)} %copy-done.2), kind=kOutput, calls=%fused_computation.48 | convolution fusion | flops 1610612736 | bytes 11272192 | tf_op jit(solution)/shard_map/esd,esf->edf/dot_general | solution.py:79
  505.0 2.9 copy.43
  507.8 5.6 %gather_fusion.1 = bf16[1024,512]{1,0:T(8,128)(2,1)S(1)} fusion(bf16[1536,512]{1,0:T(8,128)(2,1)} %bitcast.65, s32[1024]{0:T(1024)S(1)} %broadcast_clamp_fusion), kind=kCustom, calls=%fused_computation.1 | custom fusion | bytes 2101248 | tf_op jit(solution)/shard_map/gather | solution.py:105
  513.4 1.6 fusion.2
  515.0 11.1 %psum.7 = f32[128,8]{1,0:T(8,128)S(1)} all-reduce(f32[128,8]{1,0:T(8,128)S(1)} %get-tuple-element.12), channel_id=1, replica_groups=mesh['dp'=8,'et'=4] {'et'}, use_global_device_ids=true, to_apply=%region_9.10 | all-reduce | flops 1024 | bytes 8192 | tf_op jit(solution)/shard_map/psum | solution.py:118
  526.1 0.7 copy.51
  526.8 2.9 copy.47
  529.7 5.6 %gather_fusion.4 = bf16[1024,512]{1,0:T(8,128)(2,1)S(1)} fusion(bf16[1536,512]{1,0:T(8,128)(2,1)} %bitcast.64, s32[1024]{0:T(1024)S(1)} %broadcast_clamp_fusion), kind=kCustom, calls=%fused_computation.4 | custom fusion | bytes 2101248 | tf_op jit(solution)/shard_map/gather | solution.py:110
  535.3 1.3 bitcast_reduce_fusion
  (32 shorter events, 0.2 us)
Async XLA Ops:
  7.2 338.9 %copy-start = (bf16[2,256,2048]{2,1,0:T(8,128)(2,1)S(1)}, bf16[2,256,2048]{2,1,0:T(8,128)(2,1)}, u32[]{:S(2)}) copy-start(bf16[2,256,2048]{2,1,0:T(8,128)(2,1)} %param.13) | copy-start | bytes 6291460
  19.5 8.5 %copy-start.7 = (bf16[128,512]{1,0:T(8,128)(2,1)S(1)}, bf16[128,512]{1,0:T(8,128)(2,1)}, u32[]{:S(2)}) copy-start(bf16[128,512]{1,0:T(8,128)(2,1)} %param.8) | copy-start | bytes 393220
  50.3 5.9 %copy-start.8 = (bf16[128,512]{1,0:T(8,128)(2,1)S(1)}, bf16[128,512]{1,0:T(8,128)(2,1)}, u32[]{:S(2)}) copy-start(bf16[128,512]{1,0:T(8,128)(2,1)} %param.7) | copy-start | bytes 393220
  50.3 144.7 %all-to-all-start.2 = ((bf16[16,96,2048]{2,1,0:T(8,128)(2,1)}), bf16[16,96,2048]{2,1,0:T(8,128)(2,1)}, u32[]{:S(2)}, u32[]{:S(2)}) async-start(bf16[16,96,2048]{2,1,0:T(8,128)(2,1)} %fusion), calls=%async_computation.3 | async-start | bytes 12582912 | tf_op jit(solution)/shard_map/all_to_all | solution.py:57
  194.9 142.6 %all-to-all-start = ((bf16[16,96,2048]{2,1,0:T(8,128)(2,1)}), bf16[16,96,2048]{2,1,0:T(8,128)(2,1)}, u32[]{:S(2)}, u32[]{:S(2)}) async-start(bf16[16,96,2048]{2,1,0:T(8,128)(2,1)} %bitcast.74), calls=%async_computation | async-start | bytes 12582912 | tf_op jit(solution)/shard_map/all_to_all | solution.py:50
  199.7 212.6 %reduce-scatter.3.cloned.1.call-start = ((), (), s32[]{:S(2)}) async-start(), calls=%async_computation.6 | async-start | bytes 7864320 | tf_op jit(solution)/shard_map/reduce_scatter | solution.py:92
  337.5 3.5 copy-start.6
  341.0 3.2 copy-start.1
  341.1 3.2 copy-start.5
  341.1 5.1 slice-start
  344.2 2.7 slice-start.1
  355.2 118.3 %reduce-scatter.5.cloned.1.call-start = ((), (), s32[]{:S(2)}) async-start(), calls=%async_computation.7 | async-start | bytes 7864320 | tf_op jit(solution)/shard_map/reduce_scatter | solution.py:95
  355.5 3.8 copy-start.3
  416.5 61.1 %all-to-all-start.1 = ((bf16[2,768,512]{2,0,1:T(2,128)(2,1)}), bf16[2,768,512]{2,0,1:T(2,128)(2,1)}, u32[]{:S(2)}, u32[]{:S(2)}) async-start(bf16[2,768,512]{2,0,1:T(2,128)(2,1)} %copy.42), calls=%async_computation.2 | async-start | bytes 3145728 | tf_op jit(solution)/shard_map/all_to_all | solution.py:100
  477.6 5.7 %copy-start.9 = (bf16[128,8]{0,1:T(8,128)(2,1)S(1)}, bf16[128,8]{0,1:T(8,128)(2,1)}, u32[]{:S(2)}) copy-start(bf16[128,8]{0,1:T(8,128)(2,1)} %param.10) | copy-start | bytes 6148
  477.6 49.2 %all-to-all-start.3 = ((bf16[2,768,512]{2,0,1:T(2,128)(2,1)}), bf16[2,768,512]{2,0,1:T(2,128)(2,1)}, u32[]{:S(2)}, u32[]{:S(2)}) async-start(bf16[2,768,512]{2,0,1:T(2,128)(2,1)} %copy.46), calls=%async_computation.5 | async-start | bytes 3145728 | tf_op jit(solution)/shard_map/all_to_all | solution.py:101
  483.5 6.7 %copy-start.4 = (bf16[2,768,256]{2,1,0:T(8,128)(2,1)S(1)}, bf16[2,768,256]{2,1,0:T(8,128)(2,1)}, u32[]{:S(2)}) copy-start(bf16[2,768,256]{2,1,0:T(8,128)(2,1)} %get-tuple-element.14) | copy-start | bytes 2359300
  490.2 7.4 %copy-start.2 = (bf16[2,768,256]{2,1,0:T(8,128)(2,1)S(1)}, bf16[2,768,256]{2,1,0:T(8,128)(2,1)}, u32[]{:S(2)}) copy-start(bf16[2,768,256]{2,1,0:T(8,128)(2,1)} %get-tuple-element.15) | copy-start | bytes 2359300
Sparse Core Ops, SparseCore 0:
  355.3 57.0 reduce-scatter.2
  415.0 58.3 reduce-scatter.4
where the time goes:
time: 544 us
  waiting for transfers between devices  353 us (65%)
  local copies, waits for them, and re-layouts  67.8 us (12%)
  matrix products  43.8 us (8%)
  blocking collectives  26.8 us (5%)
  starting transfers between devices  22.4 us (4%)
  other arithmetic  15 us (3%)
  between operations  14.3 us (3%)
    all_to_all x1, waiting for transfers between devices, local(): lax.all_to_all(picked.reshape(experts, capacity, features), 'dp', split_a...  131 us
    all_to_all x1, waiting for transfers between devices, local(): lax.all_to_all(scaled.reshape(experts, capacity, features), 'dp', split_a...  125 us
    reduce_scatter x1, waiting for transfers between devices, local(): lax.psum_scatter(in_part.astype(jnp.bfloat16), 'et', scatter_dimension=2,...  51.4 us
    reduce_scatter x1, waiting for transfers between devices, local(): lax.psum_scatter(out_part.astype(jnp.bfloat16), 'et', scatter_dimension=2...  46.4 us
    psum x1, blocking collectives, local(): grad_gates = lax.psum(gate_part, 'et')  11.1 us
  transfers between devices with their start and end apart: 6, of which 4 were waited for; matrix products, arithmetic and copies ran while one was open for 12% of the time, Pallas kernels for 0%

commit v1 on v0

v1 whole, which is shorter than its diff:
```python
import jax
import jax.numpy as jnp
from jax import lax
from jax.sharding import PartitionSpec as P

F32 = jnp.float32
BF16 = jnp.bfloat16


def dot(a, b, ca, cb):
    return lax.dot_general(a, b, (((ca,), (cb,)), ((), ())), preferred_element_type=F32)


def piece(tokens, cotangent, expert_ids, route_gates, gate_proj, up_proj, down_proj):
    groups = lax.axis_size("dp")
    parts = lax.axis_size("et")
    mine, features, units = gate_proj.shape
    experts = mine * groups
    rows, width = tokens.shape
    total = rows * groups
    chosen = expert_ids[:, :, None] == jnp.arange(experts, dtype=jnp.int32)
    weight = jnp.sum(jnp.where(chosen, route_gates.astype(F32)[:, :, None], 0.0), axis=1)
    weights = lax.all_to_all(
        weight.reshape(rows, groups, mine).transpose(1, 0, 2), "dp", 0, 0, tiled=True
    ).reshape(total, mine)
    x = lax.all_gather(lax.all_gather(tokens, "dp", axis=0, tiled=True), "et", axis=1, tiled=True)
    c = lax.all_gather(lax.all_gather(cotangent, "dp", axis=0, tiled=True), "et", axis=1, tiled=True)
    weighted, pre_grads, inner = [], [], []
    for e in range(mine):
        g = weights[:, e : e + 1]
        pre_gate = dot(x, gate_proj[e], 1, 0)
        pre_up = dot(x, up_proj[e], 1, 0)
        back = dot(c, down_proj[e], 1, 1)
        s = jax.nn.sigmoid(pre_gate)
        silu = pre_gate * s
        hidden = silu * pre_up
        grad = back * g
        weighted.append((hidden * g).astype(BF16))
        pre_grads.append((grad * pre_up * s * (1.0 + pre_gate * (1.0 - s))).astype(BF16))
        pre_grads.append((grad * silu).astype(BF16))
        inner.append(jnp.sum(hidden * back, axis=1))
    out_part = sum(dot(weighted[e], down_proj[e], 1, 0) for e in range(mine)).astype(BF16)
    in_part = sum(
        dot(pre_grads[2 * e], gate_proj[e], 1, 1) + dot(pre_grads[2 * e + 1], up_proj[e], 1, 1)
        for e in range(mine)
    ).astype(BF16)
    sums = [
        lax.psum_scatter(
            lax.psum_scatter(part, "et", scatter_dimension=1, tiled=True),
            "dp",
            scatter_dimension=0,
            tiled=True,
        )
        for part in (out_part, in_part)
    ]
    grad_down = jnp.stack([dot(weighted[e], c, 0, 0) for e in range(mine)])
    grad_gate_w = jnp.stack([dot(x, pre_grads[2 * e], 0, 0) for e in range(mine)])
    grad_up_w = jnp.stack([dot(x, pre_grads[2 * e + 1], 0, 0) for e in range(mine)])
    inner = lax.psum(jnp.stack(inner, 1), "et").reshape(groups, rows, mine)
    inner = lax.all_to_all(inner, "dp", 0, 0, tiled=True).transpose(1, 0, 2).reshape(rows, experts)
    grad_gates = jnp.sum(jnp.where(chosen, inner[:, None, :], 0.0), axis=2)
    return (sums[0], sums[1], grad_gates, grad_gate_w, grad_up_w, grad_down)


def local(tokens, cotangent, expert_ids, route_gates, gate_proj, up_proj, down_proj):
    rows = tokens.shape[0]
    pieces = max(1, rows * lax.axis_size("dp") // 1024)
    held = (gate_proj, up_proj, down_proj)
    if pieces == 1 or rows % (16 * pieces):
        return piece(tokens, cotangent, expert_ids, route_gates, *held)

    def step(grads, part):
        done = piece(*part, *held)
        return tuple(a + b for a, b in zip(grads, done[3:])), done[:3]

    split = lambda a: a.reshape(pieces, rows // pieces, *a.shape[1:])
    grads, done = lax.scan(
        step,
        tuple(jnp.zeros(a.shape, F32) for a in held),
        tuple(split(a) for a in (tokens, cotangent, expert_ids, route_gates)),
    )
    return tuple(a.reshape(rows, *a.shape[2:]) for a in done) + grads


def solution(mesh):
    in_specs = (
        P("dp", "et"),
        P("dp", "et"),
        P("dp", None),
        P("dp", None),
        P("dp", None, "et"),
        P("dp", None, "et"),
        P("dp", "et", None),
    )
    out_specs = (
        P("dp", "et"),
        P("dp", "et"),
        P("dp", None),
        P("dp", None, "et"),
        P("dp", None, "et"),
        P("dp", "et", None),
    )
    return jax.shard_map(local, mesh=mesh, in_specs=in_specs, out_specs=out_specs, check_vma=False)
```

time: 544 us -> 458 us (0.84)
  local copies, waits for them, and re-layouts: 67.8 us -> 13.2 us
  matrix products: 43.8 us -> 60.7 us
  starting transfers between devices: 22.4 us -> 6.19 us
  waiting for transfers between devices: 353 us -> 337 us
  blocking collectives: 26.8 us -> 14.9 us
    all_to_all x4 -> x1, waiting for transfers between devices: 256 us -> 6.45 us  [piece(): lax.all_to_all(inner, 'dp', 0, 0, tiled=True).transpose(1, 0, 2)]
    all_gather x0 -> x4, waiting for transfers between devices: none -> 145 us  [the longest x1 44.3 us: piece(): lax.all_gather(tokens, 'dp', axis=0, tiled=True)]
    reduce_scatter x2 -> x4, waiting for transfers between devices: 97.8 us -> 184 us  [the longest x2 115 us: piece(): lax.psum_scatter(lax.psum_scatter(part, 'et', scatter_dimension=1, tiled=...]
    gather x5 -> x0, local copies, waits for them, and re-layouts: 33.8 us -> none  [the longest x1 8.39 us: pick_rows(): gates_ext[lookup][:, None] * cotangent_ext[holder].astype(jnp.float32)]
    dot_general x9 -> x18, matrix products: 43.8 us -> 60.7 us  [dot(): lax.dot_general(a, b, (((ca,), (cb,)), ((), ())), preferred_element_type=...]
    all_to_all x4 -> x1, starting transfers between devices: 21.9 us -> 5.66 us  [piece(): lax.all_to_all(inner, 'dp', 0, 0, tiled=True).transpose(1, 0, 2)]
    all_to_all x4 -> x0, local copies, waits for them, and re-layouts: 15.8 us -> none  [the longest x1 6.56 us: local(): lax.all_to_all(scaled.reshape(experts, capacity, features), 'dp', split_a...]
    all_gather x2 -> x0, blocking collectives: 15.7 us -> none  [the longest x1 8.65 us: local(): lax.all_gather(cotangent, 'et', axis=1, tiled=True)]
  transfers between devices with their start and end apart: 6 -> 9, of which waited for: 4 -> 9; matrix products, arithmetic and copies ran while one was open for 12% -> 11% of each run, Pallas kernels for 0% -> 0%
where the time goes in v1:
time: 458 us; the launch traced here: 457 us
  waiting for transfers between devices  337 us (74%)
  matrix products  60.7 us (13%)
  blocking collectives  14.9 us (3%)
  between operations  14.4 us (3%)
  local copies, waits for them, and re-layouts  13.2 us (3%)
  other arithmetic  10.9 us (2%)
  starting transfers between devices  6.19 us (1%)
    reduce_scatter x2, waiting for transfers between devices, piece(): lax.psum_scatter(lax.psum_scatter(part, 'et', scatter_dimension=1, tiled=...  115 us
    reduce_scatter x2, waiting for transfers between devices, piece(): lax.psum_scatter(part, 'et', scatter_dimension=1, tiled=True)  69.4 us
    dot_general x18, matrix products, dot(): lax.dot_general(a, b, (((ca,), (cb,)), ((), ())), preferred_element_type=...  60.7 us
    all_gather x1, waiting for transfers between devices, piece(): lax.all_gather(tokens, 'dp', axis=0, tiled=True)  44.3 us
    all_gather x1, waiting for transfers between devices, piece(): lax.all_gather(cotangent, 'dp', axis=0, tiled=True)  41 us
    all_gather x1, waiting for transfers between devices, piece(): lax.all_gather(lax.all_gather(tokens, 'dp', axis=0, tiled=True), 'et', ax...  34.8 us
    all_gather x1, waiting for transfers between devices, piece(): lax.all_gather(lax.all_gather(cotangent, 'dp', axis=0, tiled=True), 'et',...  24.9 us
    unnamed x39, local copies, waits for them, and re-layouts  12.6 us
  transfers between devices with their start and end apart: 9, of which 9 were waited for; matrix products, arithmetic and copies ran while one was open for 11% of the time, Pallas kernels for 0%

profile of v1, /device:TPU:0, one launch (start us, length us, event | category | flops | bytes accessed | tf_op | source)
XLA Modules:
  0.0 457.2 jit_solution(15709563023010067781)
XLA Ops:
  7.2 0.0 all-gather.5.cloned.1.call-start
  7.2 0.7 all-gather.5.cloned.1.call-update
  7.9 0.0 all-gather.9.cloned.1.call-start
  7.9 0.7 all-gather.9.cloned.1.call-update
  8.6 0.0 all-gather.7.cloned.1.call-start
  8.7 44.3 %all-gather.5.cloned.1.call-done = bf16[1024,512]{1,0:T(8,128)(2,1)} async-done(((bf16[128,512]{1,0:T(8,128)(2,1)}), bf16[1024,512]{1,0:T(8,128)(2,1)}) %all-gather.5.cloned.1.call-update) | async-done | bytes 1048592 | tf_op jit(solution)/shard_map/all_gather | solution.py:26
  53.0 0.0 all-gather.7.cloned.1.call-update
  53.0 0.0 all-gather.11.cloned.1.call-start
  53.1 41.0 %all-gather.9.cloned.1.call-done = bf16[1024,512]{1,0:T(8,128)(2,1)} async-done(((bf16[128,512]{1,0:T(8,128)(2,1)}), bf16[1024,512]{1,0:T(8,128)(2,1)}) %all-gather.9.cloned.1.call-update) | async-done | bytes 1048592 | tf_op jit(solution)/shard_map/all_gather | solution.py:27
  94.1 0.0 all-gather.11.cloned.1.call-update
  94.1 0.0 copy-start.4
  94.1 34.8 %all-gather.7.cloned.1.call-done = bf16[1024,2048]{1,0:T(8,128)(2,1)} async-done(((bf16[1024,512]{1,0:T(8,128)(2,1)}), bf16[1024,2048]{1,0:T(8,128)(2,1)}) %all-gather.7.cloned.1.call-update) | async-done | bytes 4194320 | tf_op jit(solution)/shard_map/all_gather | solution.py:26
  128.9 4.9 %fusion.4 = f32[1024,256]{0,1:T(8,128)} fusion(bf16[1024,2048]{1,0:T(8,128)(2,1)} %all-gather.7.cloned.1.call-done, bf16[2,2048,256]{2,1,0:T(8,128)(2,1)} %param.12), kind=kOutput, calls=%fused_computation.15 | convolution fusion | flops 1073741824 | bytes 6291456 | tf_op jit(solution)/shard_map/dot_general | solution.py:11
  133.8 1.3 fusion.16
  135.1 0.3 copy-done
  135.4 2.3 fusion.8
  137.7 2.3 fusion.20
  140.0 24.9 %all-gather.11.cloned.1.call-done = bf16[1024,2048]{1,0:T(8,128)(2,1)} async-done(((bf16[1024,512]{1,0:T(8,128)(2,1)}), bf16[1024,2048]{1,0:T(8,128)(2,1)}) %all-gather.11.cloned.1.call-update) | async-done | bytes 4194320 | tf_op jit(solution)/shard_map/all_gather | solution.py:27
  164.9 5.3 %multiply_reduce_fusion = (f32[1024]{0:T(1024)S(1)}, f32[1024,256]{0,1:T(8,128)}) fusion(f32[1024,256]{0,1:T(8,128)} %fusion.4, f32[1024,256]{0,1:T(8,128)} %fusion.8, bf16[1024,2048]{1,0:T(8,128)(2,1)} %all-gather.11.cloned.1.call-done, bf16[2,256,2048]{2,1,0:T(8,128)(2,1)S(1)} %copy-done.2), kind=kOutput, calls=%fused_computation.33 | convolution fusion | flops 1075575808 | bytes 8392704 | tf_op jit(solution)/shard_map/dot_general | solution.py:11
  170.2 0.0 copy-start.12
  170.2 0.0 copy-start.11
  170.2 2.4 multiply_reduce_fusion.1
  172.6 6.0 %psum.7 = f32[8,128,2]{1,0,2:T(8,128)S(1)} all-reduce(f32[8,128,2]{1,0,2:T(8,128)S(1)} %bitcast.99), channel_id=1, replica_groups=mesh['dp'=8,'et'=4] {'et'}, use_global_device_ids=true, to_apply=%region_7.8 | all-reduce | flops 2048 | bytes 16384 | tf_op jit(solution)/shard_map/psum | solution.py:59
  178.6 0.6 copy.29
  179.2 5.7 %all-to-all-start.1 = ((f32[8,128,2]{1,2,0:T(2,128)}), f32[8,128,2]{1,2,0:T(2,128)S(1)}, u32[]{:S(2)}, u32[]{:S(2)}) async-start(f32[8,128,2]{1,2,0:T(2,128)} %copy.29), calls=%async_computation.5 | async-start | bytes 16384 | tf_op jit(solution)/shard_map/all_to_all | solution.py:60
  184.9 0.0 reduce-scatter.9.cloned.1.call-start
  184.9 6.4 %all-to-all-done.1 = f32[8,128,2]{1,2,0:T(2,128)S(1)} async-done(((f32[8,128,2]{1,2,0:T(2,128)}), f32[8,128,2]{1,2,0:T(2,128)S(1)}, u32[]{:S(2)}, u32[]{:S(2)}) %all-to-all-start.1) | async-done | bytes 8224 | tf_op jit(solution)/shard_map/all_to_all | solution.py:60
  191.4 0.6 select_reduce_fusion
  192.0 8.9 %all_to_all.10 = f32[8,128,2]{1,2,0:T(2,128)S(1)} all-to-all(f32[8,128,2]{1,2,0:T(2,128)S(1)} %bitcast.97), channel_id=1, replica_groups=mesh['dp'=8,'et'=4] {'dp'}, dimensions={0} | all-to-all | bytes 16384 | tf_op jit(solution)/shard_map/all_to_all | solution.py:23
  200.9 2.6 multiply_convert_fusion
  203.5 0.0 copy-start.9
  203.6 0.0 copy-start.10
  203.6 2.7 fusion.6
  206.3 0.0 copy-start.5
  206.3 0.8 multiply_convert_fusion.2
  207.1 0.8 copy-done.5
  207.9 4.5 fusion.14
  212.4 4.6 fusion.18
  217.0 9.5 %add_convert_fusion = bf16[1024,2048]{1,0:T(8,128)(2,1)} fusion(f32[1024,2048]{1,0:T(8,128)S(1)} %fusion.6, f32[1024,2048]{1,0:T(8,128)} %fusion.18, f32[1024,2048]{1,0:T(8,128)} %fusion.14, bf16[1024,256]{0,1:T(8,128)(2,1)S(1)} %get-tuple-element.32, bf16[2,2048,256]{2,1,0:T(8,128)(2,1)} %param.12), kind=kOutput, calls=%fused_computation | convolution fusion | flops 1082130432 | bytes 30932992 | tf_op jit(solution)/shard_map/dot_general | solution.py:11
  226.4 0.0 reduce-scatter.9.cloned.1.call-update
  226.5 0.0 reduce-scatter.5.cloned.1.call-start
  226.5 0.0 copy-start.3
  226.5 2.7 fusion.12
  229.2 3.8 add_convert_fusion.1
  233.0 0.0 reduce-scatter.5.cloned.1.call-update
  233.0 0.0 reduce-scatter.11.cloned.1.call-start
  233.1 35.3 %reduce-scatter.9.cloned.1.call-done = bf16[1024,512]{1,0:T(8,128)(2,1)} async-done(((bf16[1024,2048]{1,0:T(8,128)(2,1)}), bf16[1024,512]{1,0:T(8,128)(2,1)}) %reduce-scatter.9.cloned.1.call-update) | async-done | bytes 1048592 | tf_op jit(solution)/shard_map/reduce_scatter | solution.py:49
  268.4 0.0 reduce-scatter.11.cloned.1.call-update
  268.4 0.3 reduce-scatter.7.cloned.1.call-start
  268.7 3.6 convolution_bitcast_fusion.4
  272.3 1.3 convolution_bitcast_fusion.5
  273.6 2.3 pad_maximum_fusion
  275.9 6.1 %copy.30 = f32[2,2048,256]{2,1,0:T(8,128)} copy(f32[2,2048,256]{1,2,0:T(8,128)} %pad_maximum_fusion) | data formatting | bytes 8388608
  281.9 34.1 %reduce-scatter.5.cloned.1.call-done = bf16[1024,512]{1,0:T(8,128)(2,1)} async-done(((bf16[1024,2048]{1,0:T(8,128)(2,1)}), bf16[1024,512]{1,0:T(8,128)(2,1)}) %reduce-scatter.5.cloned.1.call-update) | async-done | bytes 1048592 | tf_op jit(solution)/shard_map/reduce_scatter | solution.py:49
  316.1 0.0 reduce-scatter.7.cloned.1.call-update
  316.1 3.6 convolution_bitcast_fusion.2
  319.7 1.3 convolution_bitcast_fusion.3
  321.0 2.3 pad_maximum_fusion.1
  323.3 5.3 %copy.31 = f32[2,2048,256]{2,1,0:T(8,128)} copy(f32[2,2048,256]{1,2,0:T(8,128)} %pad_maximum_fusion.1) | data formatting | bytes 8388608
  328.6 3.6 convolution_bitcast_fusion
  332.2 1.3 convolution_bitcast_fusion.1
  333.5 2.3 pad_maximum_fusion.2
  335.8 47.7 %reduce-scatter.11.cloned.1.call-done = bf16[128,512]{1,0:T(8,128)(2,1)} async-done(((bf16[1024,512]{1,0:T(8,128)(2,1)}), bf16[128,512]{1,0:T(8,128)(2,1)}) %reduce-scatter.11.cloned.1.call-update) | async-done | bytes 131088 | tf_op jit(solution)/shard_map/reduce_scatter | solution.py:48
  383.5 66.9 %reduce-scatter.7.cloned.1.call-done = bf16[128,512]{1,0:T(8,128)(2,1)} async-done(((bf16[1024,512]{1,0:T(8,128)(2,1)}), bf16[128,512]{1,0:T(8,128)(2,1)}) %reduce-scatter.7.cloned.1.call-update) | async-done | bytes 131088 | tf_op jit(solution)/shard_map/reduce_scatter | solution.py:48
  (31 shorter events, 0.1 us)
Async XLA Ops:
  7.2 45.8 %all-gather.5.cloned.1.call-start = ((), (), s32[]{:S(2)}) async-start(), calls=%async_computation.6 | async-start | bytes 1179648 | tf_op jit(solution)/shard_map/all_gather | solution.py:26
  7.9 86.2 %all-gather.9.cloned.1.call-start = ((), (), s32[]{:S(2)}) async-start(), calls=%async_computation.10 | async-start | bytes 1179648 | tf_op jit(solution)/shard_map/all_gather | solution.py:27
  8.6 120.3 %all-gather.7.cloned.1.call-start = ((), (), s32[]{:S(2)}) async-start(), calls=%async_computation.7 | async-start | bytes 5242880 | tf_op jit(solution)/shard_map/all_gather | solution.py:26
  53.0 111.8 %all-gather.11.cloned.1.call-start = ((), (), s32[]{:S(2)}) async-start(), calls=%async_computation.11 | async-start | bytes 5242880 | tf_op jit(solution)/shard_map/all_gather | solution.py:27
  94.1 39.7 %copy-start.4 = (bf16[2,2048,256]{2,1,0:T(8,128)(2,1)S(1)}, bf16[2,2048,256]{2,1,0:T(8,128)(2,1)}, u32[]{:S(2)}) copy-start(bf16[2,2048,256]{2,1,0:T(8,128)(2,1)} %param.12) | copy-start | bytes 6291460
  128.9 4.9 %copy-start.13 = (bf16[1024,2048]{1,0:T(8,128)(2,1)S(1)}, bf16[1024,2048]{1,0:T(8,128)(2,1)}, u32[]{:S(2)}) copy-start(bf16[1024,2048]{1,0:T(8,128)(2,1)} %all-gather.7.cloned.1.call-done) | copy-start | bytes 12582916
  133.8 1.6 copy-start
  135.4 34.7 %copy-start.6 = (f32[1024,256]{0,1:T(8,128)}, f32[1024,256]{0,1:T(8,128)S(1)}, u32[]{:S(2)}) copy-start(f32[1024,256]{0,1:T(8,128)S(1)} %fusion.16) | copy-start | bytes 3145732
  137.7 27.2 %copy-start.2 = (bf16[2,256,2048]{2,1,0:T(8,128)(2,1)S(1)}, bf16[2,256,2048]{2,1,0:T(8,128)(2,1)}, u32[]{:S(2)}) copy-start(bf16[2,256,2048]{2,1,0:T(8,128)(2,1)} %param.13) | copy-start | bytes 6291460
  164.9 5.3 %copy-start.8 = (f32[1024,256]{0,1:T(8,128)S(1)}, f32[1024,256]{0,1:T(8,128)}, u32[]{:S(2)}) copy-start(f32[1024,256]{0,1:T(8,128)} %fusion.20) | copy-start | bytes 3145732
  164.9 5.3 %copy-start.16 = (bf16[1024,2048]{1,0:T(8,128)(2,1)S(1)}, bf16[1024,2048]{1,0:T(8,128)(2,1)}, u32[]{:S(2)}) copy-start(bf16[1024,2048]{1,0:T(8,128)(2,1)} %all-gather.11.cloned.1.call-done) | copy-start | bytes 12582916
  170.2 14.8 %copy-start.12 = (bf16[128,8]{0,1:T(8,128)(2,1)S(1)}, bf16[128,8]{0,1:T(8,128)(2,1)}, u32[]{:S(2)}) copy-start(bf16[128,8]{0,1:T(8,128)(2,1)} %param.10) | copy-start | bytes 6148
  170.2 21.2 %copy-start.11 = (s32[128,8]{0,1:T(8,128)S(1)}, s32[128,8]{0,1:T(8,128)}, u32[]{:S(2)}) copy-start(s32[128,8]{0,1:T(8,128)} %param.9) | copy-start | bytes 12292
  179.2 12.2 %all-to-all-start.1 = ((f32[8,128,2]{1,2,0:T(2,128)}), f32[8,128,2]{1,2,0:T(2,128)S(1)}, u32[]{:S(2)}, u32[]{:S(2)}) async-start(f32[8,128,2]{1,2,0:T(2,128)} %copy.29), calls=%async_computation.5 | async-start | bytes 16384 | tf_op jit(solution)/shard_map/all_to_all | solution.py:60
  184.9 83.5 %reduce-scatter.9.cloned.1.call-start = ((), (), s32[]{:S(2)}) async-start(), calls=%async_computation.12 | async-start | bytes 5242880 | tf_op jit(solution)/shard_map/reduce_scatter | solution.py:49
  203.5 2.7 copy-start.7
  203.5 2.7 copy-start.9
  203.6 2.7 copy-start.10
  206.3 1.6 copy-start.5
  207.9 4.5 copy-start.1
  226.5 89.6 %reduce-scatter.5.cloned.1.call-start = ((), (), s32[]{:S(2)}) async-start(), calls=%async_computation.8 | async-start | bytes 5242880 | tf_op jit(solution)/shard_map/reduce_scatter | solution.py:49
  226.5 2.7 copy-start.3
  233.0 150.5 %reduce-scatter.11.cloned.1.call-start = ((), (), s32[]{:S(2)}) async-start(), calls=%async_computation.13 | async-start | bytes 1179648 | tf_op jit(solution)/shard_map/reduce_scatter | solution.py:48
  268.4 182.0 %reduce-scatter.7.cloned.1.call-start = ((), (), s32[]{:S(2)}) async-start(), calls=%async_computation.9 | async-start | bytes 1179648 | tf_op jit(solution)/shard_map/reduce_scatter | solution.py:48
  268.7 3.6 copy-start.14
  316.1 3.6 copy-start.15
  328.6 3.6 copy-start.17
Sparse Core Ops, SparseCore 0:
  10.1 42.8 all-gather.4
  55.1 38.8 all-gather.8
  95.6 33.2 all-gather.6
  130.3 34.4 all-gather.10
  226.6 41.7 reduce-scatter.8
  271.5 44.5 reduce-scatter.4
  320.0 63.4 reduce-scatter.10
  387.9 62.4 reduce-scatter.6

commit v2 on v1

--- a/solution.py
+++ b/solution.py
@@ -1,30 +1,285 @@
+import functools
+import itertools
 import jax
 import jax.numpy as jnp
 from jax import lax
+from jax.experimental import pallas as pl
+from jax.experimental.pallas import tpu as pltpu
 from jax.sharding import PartitionSpec as P
 
 F32 = jnp.float32
 BF16 = jnp.bfloat16
 
 
+def sizes():
+    groups, parts = lax.axis_size("dp"), lax.axis_size("et")
+    across = 2 if groups <= 8 else 4
+    return {"z": groups // across, "x": across, "y": parts // 2, "c": 2}
+
+
+def position(size):
+    dp, et = lax.axis_index("dp"), lax.axis_index("et")
+    return {"z": dp // size["x"], "x": dp % size["x"], "y": et // 2, "c": et % 2}
+
+
+def device(size, at):
+    return (at["z"] * size["x"] + at["x"], at["y"] * 2 + at["c"])
+
+
+def beside(size, at, axis, step):
+    return {**at, axis: lax.rem(at[axis] + step, size[axis])}
+
+
+def greet(size, me):
+    barrier = pltpu.get_barrier_semaphore()
+    count = 0
+    for axis in size:
+        for step in range(1, size[axis]):
+            pl.semaphore_signal(
+                barrier,
+                inc=1,
+                device_id=device(size, beside(size, me, axis, step)),
+                device_id_type=pl.DeviceIdType.MESH,
+            )
+            count += 1
+    pl.semaphore_wait(barrier, count)
+
+
+def block(ref, size, at):
+    rows, width = (ref.shape[0] // (size["z"] * size["x"]), ref.shape[1] // (size["y"] * 2))
+    dp, et = device(size, at)
+    return ref.at[
+        pl.ds(pl.multiple_of(dp * rows, rows), rows),
+        pl.ds(pl.multiple_of(et * width, width), width),
+    ]
+
+
+ORDERS = (("z", "x", "y", "c"), ("z", "y", "x", "c"))
+
+
+def gather_kernel(size, t_ref, c_ref, w_ref, x_out, c_out, w_out, own, sends, recvs):
+    me = position(size)
+    greet(size, me)
+    sources = (t_ref, c_ref, w_ref)
+    targets = (x_out, c_out, w_out)
+    orders = ORDERS + (("z", "x"),)
+
+    def place(t, at):
+        if t < 2:
+            return block(targets[t], size, at)
+        rows = w_ref.shape[0]
+        dp = device(size, at)[0]
+        return w_out.at[pl.ds(pl.multiple_of(dp * rows, rows), rows), :]
+
+    def index(at):
+        dp, et = device(size, at)
+        return dp * (size["y"] * 2) + et
+
+    started = []
+
+    def forward(t, at, source, stage):
+        for axis in orders[t][stage:]:
+            for step in range(1, size[axis]):
+                copy = pltpu.make_async_remote_copy(
+                    src_ref=source,
+                    dst_ref=place(t, at),
+                    send_sem=sends.at[len(started)],
+                    recv_sem=recvs.at[t, index(at)],
+                    device_id=device(size, beside(size, me, axis, step)),
+                    device_id_type=pl.DeviceIdType.MESH,
+                )
+                copy.start()
+                started.append(copy)
+
+    for t in (2, 0, 1):
+        forward(t, me, sources[t], 0)
+    kept = []
+    for t in range(3):
+        copy = pltpu.make_async_copy(sources[t], place(t, me), own.at[t])
+        copy.start()
+        kept.append(copy)
+    for stage in range(4):
+        lists = []
+        for t in (2, 0, 1):
+            order = orders[t]
+            if stage >= len(order):
+                continue
+            axis = order[stage]
+            steps = [range(size[a]) for a in order[:stage]] + [range(1, size[axis])]
+            lists.append([(t, tuple(zip(order, walk))) for walk in itertools.product(*steps)])
+        for group in itertools.zip_longest(*lists):
+            for item in group:
+                if item is None:
+                    continue
+                t, walk = item
+                at = dict(me)
+                for axis, step in walk:
+                    at = beside(size, at, axis, step) if step else at
+                pltpu.make_async_copy(place(t, at), place(t, at), recvs.at[t, index(at)]).wait()
+                forward(t, at, place(t, at), stage + 1)
+    for copy in kept:
+        copy.wait()
+    for copy in started:
+        copy.wait_send()
+
+
+def gather(tokens, cotangent, weight):
+    size = sizes()
+    groups, parts = size["z"] * size["x"], size["y"] * 2
+    rows, width = tokens.shape
+    whole = jax.ShapeDtypeStruct((rows * groups, width * parts), BF16)
+    anywhere = pl.BlockSpec(memory_space=pl.ANY)
+    copies = 2 * (groups * parts - 1) + groups - 1
+    return pl.pallas_call(
+        functools.partial(gather_kernel, size),
+        out_shape=(whole, whole, jax.ShapeDtypeStruct((rows * groups, weight.shape[1]), BF16)),
+        in_specs=[anywhere] * 3,
+        out_specs=[anywhere] * 3,
+        scratch_shapes=[
+            pltpu.SemaphoreType.DMA((3,)),
+            pltpu.SemaphoreType.DMA((copies,)),
+            pltpu.SemaphoreType.DMA((3, groups * parts)),
+        ],
+        compiler_params=pltpu.CompilerParams(collective_id=0, has_side_effects=True),
+        name="gather",
+    )(tokens, cotangent, weight)
+
+
+def scatter_kernel(size, m_ref, g_ref, m_out, g_out, first, second0, second1, third0, third1,
+                   last, sends, r0, r1, r2, r3):
+    me = position(size)
+    greet(size, me)
+    parts = (m_ref, g_ref)
+    outs = (m_out, g_out)
+    seconds, thirds = (second0, second1), (third0, third1)
+    orders = (("y", "x"), ("x", "y"))
+    started = []
+
+    def send(source, target, recv, axis, step):
+        copy = pltpu.make_async_remote_copy(
+            src_ref=source,
+            dst_ref=target,
+            send_sem=sends.at[len(started)],
+            recv_sem=recv,
+            device_id=device(size, beside(size, me, axis, step)),
+            device_id_type=pl.DeviceIdType.MESH,
+        )
+        copy.start()
+        started.append(copy)
+
+    def arrived(ref, sem):
+        pltpu.make_async_copy(ref, ref, sem).wait()
+
+    def along(t, a, b, k):
+        at = dict(me)
+        for axis, step in zip(orders[t] + ("z",), (a, b, k)):
+            at = beside(size, at, axis, step) if step else at
+        return at
+
+    walks = []
+    for t in range(2):
+        na, nb = (size[axis] for axis in orders[t])
+        walks.append(
+            [(a, b, k) for a in reversed(range(na)) for b in reversed(range(nb))
+             for k in reversed(range(size["z"]))]
+        )
+    for walk0, walk1 in zip(*walks):
+        for t, walk in ((0, walk0), (1, walk1)):
+            n = walks[t].index(walk)
+            to = beside(size, along(t, *walk), "c", 1)
+            send(block(parts[t], size, to), first.at[t, n], r0.at[t, n], "c", 1)
+    for i in range(len(walks[0])):
+        for t in range(2):
+            a, b, k = walks[t][i]
+            arrived(first.at[t, i], r0.at[t, i])
+            own = block(parts[t], size, along(t, a, b, k))
+            first[t, i] = (first[t, i].astype(F32) + own[...].astype(F32)).astype(BF16)
+            if a:
+                slot = b * size["z"] + k
+                send(first.at[t, i], seconds[t].at[a - 1, slot], r1.at[t, a - 1, slot], orders[t][0], a)
+    pairs = [
+        [(b, k) for b in reversed(range(size[orders[t][1]])) for k in reversed(range(size["z"]))]
+        for t in range(2)
+    ]
+    for i in range(len(pairs[0])):
+        for t in range(2):
+            b, k = pairs[t][i]
+            slot = b * size["z"] + k
+            n = walks[t].index((0, b, k))
+            total = first[t, n].astype(F32)
+            for d in range(size[orders[t][0]] - 1):
+                arrived(seconds[t].at[d, slot], r1.at[t, d, slot])
+                total = total + seconds[t][d, slot].astype(F32)
+            seconds[t][0, slot] = total.astype(BF16)
+            if b:
+                send(seconds[t].at[0, slot], thirds[t].at[b - 1, k], r2.at[t, b - 1, k], orders[t][1], b)
+    for k in reversed(range(size["z"])):
+        for t in range(2):
+            total = seconds[t][0, k].astype(F32)
+            for d in range(size[orders[t][1]] - 1):
+                arrived(thirds[t].at[d, k], r2.at[t, d, k])
+                total = total + thirds[t][d, k].astype(F32)
+            thirds[t][0, k] = total.astype(BF16)
+            if k:
+                send(thirds[t].at[0, k], last.at[t, k - 1], r3.at[t, k - 1], "z", k)
+    for t in range(2):
+        total = thirds[t][0, 0].astype(F32)
+        for d in range(size["z"] - 1):
+            arrived(last.at[t, d], r3.at[t, d])
+            total = total + last[t, d].astype(F32)
+        outs[t][...] = total.astype(BF16)
+    for copy in started:
+        copy.wait_send()
+
+
+def scatter(out_part, in_part):
+    size = sizes()
+    nz, nx, ny = size["z"], size["x"], size["y"]
+    rows, width = out_part.shape[0] // (nz * nx), out_part.shape[1] // (ny * 2)
+    one = jax.ShapeDtypeStruct((rows, width), BF16)
+    inside = pl.BlockSpec(memory_space=pltpu.VMEM)
+    dma = pltpu.SemaphoreType.DMA
+    wide = max(nx, ny)
+    return pl.pallas_call(
+        functools.partial(scatter_kernel, size),
+        out_shape=(one, one),
+        in_specs=[inside] * 2,
+        out_specs=[inside] * 2,
+        scratch_shapes=[
+            pltpu.VMEM((2, nz * nx * ny, rows, width), BF16),
+            pltpu.VMEM((ny - 1, nx * nz, rows, width), BF16),
+            pltpu.VMEM((nx - 1, ny * nz, rows, width), BF16),
+            pltpu.VMEM((nx - 1, nz, rows, width), BF16),
+            pltpu.VMEM((ny - 1, nz, rows, width), BF16),
+            pltpu.VMEM((2, nz - 1, rows, width), BF16),
+            dma((4 * nz * nx * ny + 2 * nz,)),
+            dma((2, nz * nx * ny)),
+            dma((2, wide - 1, wide * nz)),
+            dma((2, wide - 1, nz)),
+            dma((2, nz - 1)),
+        ],
+        compiler_params=pltpu.CompilerParams(
+            collective_id=1, has_side_effects=True, vmem_limit_bytes=40 * 2**20
+        ),
+        name="scatter",
+    )(out_part, in_part)
+
+
 def dot(a, b, ca, cb):
     return lax.dot_general(a, b, (((ca,), (cb,)), ((), ())), preferred_element_type=F32)
 
 
 def piece(tokens, cotangent, expert_ids, route_gates, gate_proj, up_proj, down_proj):
     groups = lax.axis_size("dp")
-    parts = lax.axis_size("et")
     mine, features, units = gate_proj.shape
     experts = mine * groups
     rows, width = tokens.shape
     total = rows * groups
     chosen = expert_ids[:, :, None] == jnp.arange(experts, dtype=jnp.int32)
     weight = jnp.sum(jnp.where(chosen, route_gates.astype(F32)[:, :, None], 0.0), axis=1)
-    weights = lax.all_to_all(
-        weight.reshape(rows, groups, mine).transpose(1, 0, 2), "dp", 0, 0, tiled=True
-    ).reshape(total, mine)
-    x = lax.all_gather(lax.all_gather(tokens, "dp", axis=0, tiled=True), "et", axis=1, tiled=True)
-    c = lax.all_gather(lax.all_gather(cotangent, "dp", axis=0, tiled=True), "et", axis=1, tiled=True)
+    lanes = -experts % 128
+    x, c, weights = gather(tokens, cotangent, jnp.pad(weight, ((0, 0), (0, lanes))).astype(BF16))
+    weights = lax.dynamic_slice_in_dim(weights, lax.axis_index("dp") * mine, mine, 1).astype(F32)
     weighted, pre_grads, inner = [], [], []
     for e in range(mine):
         g = weights[:, e : e + 1]
@@ -44,15 +299,7 @@
         dot(pre_grads[2 * e], gate_proj[e], 1, 1) + dot(pre_grads[2 * e + 1], up_proj[e], 1, 1)
         for e in range(mine)
     ).astype(BF16)
-    sums = [
-        lax.psum_scatter(
-            lax.psum_scatter(part, "et", scatter_dimension=1, tiled=True),
-            "dp",
-            scatter_dimension=0,
-            tiled=True,
-        )
-        for part in (out_part, in_part)
-    ]
+    sums = lax.optimization_barrier(scatter(out_part, in_part))
     grad_down = jnp.stack([dot(weighted[e], c, 0, 0) for e in range(mine)])
     grad_gate_w = jnp.stack([dot(x, pre_grads[2 * e], 0, 0) for e in range(mine)])
     grad_up_w = jnp.stack([dot(x, pre_grads[2 * e + 1], 0, 0) for e in range(mine)])

time: 458 us -> 209 us (0.46)
  waiting for transfers between devices: 337 us -> 0.01 us
  Pallas kernels: 0 us -> 111 us
  between operations: 14.4 us -> 0.84 us
  local copies, waits for them, and re-layouts: 13.2 us -> 3.55 us
  blocking collectives: 14.9 us -> 7.83 us
  starting transfers between devices: 6.19 us -> 11 us
    reduce_scatter x4 -> x0, waiting for transfers between devices: 184 us -> none  [the longest x2 115 us: piece(): lax.psum_scatter(lax.psum_scatter(part, 'et', scatter_dimension=1, tiled=...]
    all_gather x4 -> x0, waiting for transfers between devices: 145 us -> none  [the longest x1 44.3 us: piece(): lax.all_gather(tokens, 'dp', axis=0, tiled=True)]
    pallas_call x0 -> x2, Pallas kernels: none -> 111 us  [the longest x1 56.8 us: scatter(): pl.pallas_call(functools.partial(scatter_kernel, size), out_shape=(one, o...]
    unnamed x39 -> x37, local copies, waits for them, and re-layouts: 12.6 us -> 1.69 us
    all_to_all x1 -> x0, blocking collectives: 8.87 us -> none  [piece(): lax.all_to_all(weight.reshape(rows, groups, mine).transpose(1, 0, 2), 'dp...]
    all_to_all x1, waiting for transfers between devices: 6.45 us -> 0.01 us  [piece(): lax.all_to_all(inner, 'dp', 0, 0, tiled=True).transpose(1, 0, 2)]
    all_to_all x1, starting transfers between devices: 5.66 us -> 11 us  [piece(): lax.all_to_all(inner, 'dp', 0, 0, tiled=True).transpose(1, 0, 2)]
    another operation x1, other arithmetic: 2.29 us -> 7.4 us  [piece(): jnp.stack([dot(x, pre_grads[2 * e], 0, 0) for e in range(mine)])]
  transfers between devices with their start and end apart: 9 -> 1, of which waited for: 9 -> 0; matrix products, arithmetic and copies ran while one was open for 11% -> 25% of each run, Pallas kernels for 0% -> 27%
where the time goes in v2:
time: 209 us; the launch traced here: 208 us
  Pallas kernels  111 us (53%)
  matrix products  62.3 us (30%)
  other arithmetic  11.8 us (6%)
  starting transfers between devices  11 us (5%)
  blocking collectives  7.83 us (4%)
  local copies, waits for them, and re-layouts  3.55 us (2%)
    dot_general x18, matrix products, dot(): lax.dot_general(a, b, (((ca,), (cb,)), ((), ())), preferred_element_type=...  62.3 us
    pallas_call x1, Pallas kernels, scatter(): pl.pallas_call(functools.partial(scatter_kernel, size), out_shape=(one, o...  56.8 us
    pallas_call x1, Pallas kernels, gather(): pl.pallas_call(functools.partial(gather_kernel, size), out_shape=(whole,...  53.9 us
    all_to_all x1, starting transfers between devices, piece(): lax.all_to_all(inner, 'dp', 0, 0, tiled=True).transpose(1, 0, 2)  11 us
    psum x1, blocking collectives, piece(): inner = lax.psum(jnp.stack(inner, 1), 'et').reshape(groups, rows, mine)  7.83 us
    another operation x1, other arithmetic, piece(): jnp.stack([dot(x, pre_grads[2 * e], 0, 0) for e in range(mine)])  7.4 us
  transfers between devices with their start and end apart: 1, of which 0 were waited for; matrix products, arithmetic and copies ran while one was open for 25% of the time, Pallas kernels for 27%

profile of v2, /device:TPU:0, one launch (start us, length us, event | category | flops | bytes accessed | tf_op | source)
XLA Modules:
  0.0 208.1 jit_solution(14017547115887198675)
XLA Ops:
  0.6 0.7 convert_element_type.33
  1.3 0.7 select_reduce_fusion.1
  2.0 0.1 copy.25
  2.1 0.6 pad.5.w_ref
  2.8 53.9 %gather.1 = (bf16[1024,2048]{1,0:T(8,128)(2,1)}, bf16[1024,2048]{1,0:T(8,128)(2,1)}, bf16[1024,128]{1,0:T(8,128)(2,1)}) custom-call(bf16[128,512]{1,0:T(8,128)(2,1)} %t_ref.1, bf16[128,512]{1,0:T(8,128)(2,1)} %c_ref.1, bf16[128,128]{1,0:T(8,128)(2,1)} %pad.5.w_ref), custom_call_target="tpu_custom_call" | custom-call | tf_op jit(solution)/shard_map/gather/pallas_call | solution.py:133
  56.7 0.0 copy-start.3
  56.7 0.0 copy-start.13
  56.7 4.9 %fusion.4 = f32[1024,256]{0,1:T(8,128)} fusion(bf16[1024,2048]{1,0:T(8,128)(2,1)} %get-tuple-element.11, bf16[2,2048,256]{2,1,0:T(8,128)(2,1)} %param.12), kind=kOutput, calls=%fused_computation.15 | convolution fusion | flops 1073741824 | bytes 6291456 | tf_op jit(solution)/shard_map/dot_general | solution.py:269
  61.6 0.0 copy-done.3
  61.6 0.0 copy-done.13
  61.7 0.0 copy-start
  61.7 2.3 %fusion.16 = f32[1024,256]{0,1:T(8,128)} fusion(bf16[1024,2048]{1,0:T(8,128)(2,1)S(1)} %copy-done.13, bf16[2,2048,256]{2,1,0:T(8,128)(2,1)S(1)} %copy-done.3), kind=kOutput, calls=%fused_computation.27 | convolution fusion | flops 1073741824 | bytes 6291456 | tf_op jit(solution)/shard_map/dot_general | solution.py:269
  63.9 0.0 copy-done
  63.9 2.3 %fusion.8 = f32[1024,256]{0,1:T(8,128)} fusion(bf16[1024,2048]{1,0:T(8,128)(2,1)S(1)} %copy-done.13, bf16[2,2048,256]{2,1,0:T(8,128)(2,1)S(1)} %copy-done), kind=kOutput, calls=%fused_computation.19 | convolution fusion | flops 1073741824 | bytes 6291456 | tf_op jit(solution)/shard_map/dot_general | solution.py:269
  66.2 0.0 copy-start.9
  66.2 2.3 %fusion.20 = f32[1024,256]{0,1:T(8,128)} fusion(bf16[1024,2048]{1,0:T(8,128)(2,1)S(1)} %copy-done.13, bf16[2,2048,256]{2,1,0:T(8,128)(2,1)S(1)} %copy-done), kind=kOutput, calls=%fused_computation.31 | convolution fusion | flops 1073741824 | bytes 6291456 | tf_op jit(solution)/shard_map/dot_general | solution.py:269
  68.5 0.0 copy-done.9
  68.5 0.1 dynamic-slice_convert_fusion
  68.6 0.5 slice_reduce_fusion
  69.1 0.0 copy-start.1
  69.1 0.0 copy-start.11
  69.1 0.0 copy-start.15
  69.1 0.0 copy-start.16
  69.2 6.0 %multiply_reduce_fusion = (f32[1024]{0:T(1024)S(1)}, bf16[1024,256]{0,1:T(8,128)(2,1)S(1)}, bf16[1024,256]{0,1:T(8,128)(2,1)}, bf16[1024,256]{0,1:T(8,128)(2,1)}) fusion(f32[1024,256]{0,1:T(8,128)} %fusion.4, f32[1024,256]{0,1:T(8,128)} %fusion.8, f32[1024]{0:T(1024)S(1)} %get-tuple-element.16, bf16[1024,2048]{1,0:T(8,128)(2,1)} %get-tuple-element.13, ...), kind=kOutput, calls=%fused_computation.33 | convolution fusion | flops 1078721536 | bytes 8921088 | tf_op jit(solution)/shard_map/dot_general | solution.py:269
  75.1 0.0 copy-done.1
  75.1 0.0 copy-done.11
  75.1 0.0 copy-done.15
  75.1 0.0 copy-done.16
  75.2 2.8 %multiply_reduce_fusion.1 = (f32[1024]{0:T(1024)S(1)}, bf16[1024,256]{0,1:T(8,128)(2,1)}, bf16[1024,256]{0,1:T(8,128)(2,1)S(1)}, bf16[1024,256]{0,1:T(8,128)(2,1)}) fusion(f32[1024,256]{0,1:T(8,128)S(1)} %copy-done.15, f32[1024,256]{0,1:T(8,128)S(1)} %copy-done.16, f32[1024]{0:T(1024)S(1)} %get-tuple-element.17, bf16[1024,2048]{1,0:T(8,128)(2,1)S(1)} %copy-done.11, ...), kind=kOutput, calls=%fused_computation.34 | convolution fusion | flops 1078721536 | bytes 8921088 | tf_op jit(solution)/shard_map/dot_general | solution.py:269
  78.0 7.8 %psum.7 = f32[8,128,2]{1,0,2:T(8,128)S(1)} all-reduce(f32[8,128,2]{1,0,2:T(8,128)S(1)} %bitcast.83), channel_id=1, replica_groups=mesh['dp'=8,'et'=4] {'et'}, use_global_device_ids=true, to_apply=%region_3.4 | all-reduce | flops 2048 | bytes 16384 | tf_op jit(solution)/shard_map/psum | solution.py:306
  85.9 0.6 copy.26
  86.5 11.0 %all-to-all-start = ((f32[8,128,2]{1,2,0:T(2,128)}), f32[8,128,2]{1,2,0:T(2,128)S(1)}, u32[]{:S(2)}, u32[]{:S(2)}) async-start(f32[8,128,2]{1,2,0:T(2,128)} %copy.26), calls=%async_computation | async-start | bytes 16384 | tf_op jit(solution)/shard_map/all_to_all | solution.py:307
  97.4 4.8 %convolution_bitcast_fusion.4 = f32[1,2048,256]{2,1,0:T(8,128)} fusion(bf16[1024,2048]{1,0:T(8,128)(2,1)} %get-tuple-element.11, bf16[1024,256]{0,1:T(8,128)(2,1)S(1)} %get-tuple-element.21), kind=kOutput, calls=%fused_computation.9 | convolution fusion | flops 1073741824 | bytes 6815744 | tf_op jit(solution)/shard_map/dot_general | solution.py:269
  102.3 0.0 copy-start.6
  102.3 0.0 copy-start.14
  102.3 4.5 %fusion.6 = f32[1024,2048]{1,0:T(8,128)} fusion(bf16[1024,256]{0,1:T(8,128)(2,1)S(1)} %get-tuple-element.21, bf16[2,2048,256]{2,1,0:T(8,128)(2,1)S(1)} %copy-done), kind=kOutput, calls=%fused_computation.17 | convolution fusion | flops 1073741824 | bytes 9961472 | tf_op jit(solution)/shard_map/dot_general | solution.py:269
  106.8 0.0 copy-start.4
  106.8 0.0 copy-done.6
  106.8 0.0 copy-done.14
  106.8 2.7 %convolution_bitcast_fusion.3 = f32[1,2048,256]{2,1,0:T(8,128)} fusion(bf16[1024,2048]{1,0:T(8,128)(2,1)S(1)} %copy-done.14, bf16[1024,256]{0,1:T(8,128)(2,1)S(1)} %copy-done.6), kind=kOutput, calls=%fused_computation.8 | convolution fusion | flops 1073741824 | bytes 6815744 | tf_op jit(solution)/shard_map/dot_general | solution.py:269
  109.5 0.0 copy-done.4
  109.5 4.5 %fusion.14 = f32[1024,2048]{1,0:T(8,128)} fusion(bf16[1024,256]{0,1:T(8,128)(2,1)S(1)} %copy-done.6, bf16[2,2048,256]{2,1,0:T(8,128)(2,1)S(1)} %copy-done.4), kind=kOutput, calls=%fused_computation.25 | convolution fusion | flops 1073741824 | bytes 9961472 | tf_op jit(solution)/shard_map/dot_general | solution.py:269
  114.1 0.0 copy-done.5
  114.1 2.7 %convolution_bitcast_fusion.5 = f32[1,2048,256]{2,1,0:T(8,128)} fusion(bf16[1024,2048]{1,0:T(8,128)(2,1)S(1)} %copy-done.14, bf16[1024,256]{0,1:T(8,128)(2,1)S(1)} %copy-done.5), kind=kOutput, calls=%fused_computation.10 | convolution fusion | flops 1073741824 | bytes 6815744 | tf_op jit(solution)/shard_map/dot_general | solution.py:269
  116.8 4.5 %fusion.18 = f32[1024,2048]{1,0:T(8,128)} fusion(bf16[1024,256]{0,1:T(8,128)(2,1)S(1)} %copy-done.5, bf16[2,2048,256]{2,1,0:T(8,128)(2,1)S(1)} %copy-done), kind=kOutput, calls=%fused_computation.29 | convolution fusion | flops 1073741824 | bytes 9961472 | tf_op jit(solution)/shard_map/dot_general | solution.py:269
  121.3 0.0 copy-done.12
  121.3 1.3 convolution_bitcast_fusion.1
  122.6 0.3 copy-done.2
  122.9 1.3 fusion.12
  124.2 0.0 copy-start.8
  124.2 0.0 copy-done.7
  124.2 2.7 %convolution_bitcast_fusion.2 = f32[1,2048,256]{2,1,0:T(8,128)} fusion(bf16[1024,2048]{1,0:T(8,128)(2,1)S(1)} %copy-done.14, bf16[1024,256]{0,1:T(8,128)(2,1)S(1)} %copy-done.7), kind=kOutput, calls=%fused_computation.7 | convolution fusion | flops 1073741824 | bytes 6815744 | tf_op jit(solution)/shard_map/dot_general | solution.py:269
  126.9 0.0 copy-done.8
  126.9 1.5 convolution_bitcast_fusion
  128.5 1.3 add_convert_fusion.1.m_ref
  129.8 9.9 %add_convert_fusion.g_ref = bf16[1024,2048]{1,0:T(8,128)(2,1)S(1)} fusion(f32[1024,2048]{1,0:T(8,128)} %fusion.6, f32[1024,2048]{1,0:T(8,128)} %fusion.18, f32[1024,2048]{1,0:T(8,128)} %fusion.14, bf16[1024,256]{0,1:T(8,128)(2,1)S(1)} %copy-done.7, bf16[2,2048,256]{2,1,0:T(8,128)(2,1)} %param.12), kind=kOutput, calls=%fused_computation | convolution fusion | flops 1082130432 | bytes 30932992 | tf_op jit(solution)/shard_map/dot_general | solution.py:269
  139.6 7.4 %pad_maximum_fusion = (f32[2,2048,256]{2,1,0:T(8,128)}, f32[2,2048,256]{2,1,0:T(8,128)}) fusion(f32[1,2048,256]{2,1,0:T(8,128)} %convolution_bitcast_fusion.4, f32[1,2048,256]{2,1,0:T(8,128)} %convolution_bitcast_fusion.5, f32[1,2048,256]{2,1,0:T(8,128)} %convolution_bitcast_fusion.2, f32[1,2048,256]{2,1,0:T(8,128)} %convolution_bitcast_fusion.3), kind=kLoop, calls=%fused_computation.2 | loop fusion | flops 2097152 | bytes 16777216 | tf_op jit(solution)/shard_map/stack | solution.py:304
  147.0 2.3 %pad_maximum_fusion.2 = f32[2,256,2048]{2,1,0:T(8,128)} fusion(f32[1,256,2048]{2,1,0:T(8,128)S(1)} %convolution_bitcast_fusion, f32[1,256,2048]{2,1,0:T(8,128)S(1)} %convolution_bitcast_fusion.1), kind=kLoop, calls=%fused_computation.4 | loop fusion | flops 1048576 | bytes 8388608 | tf_op jit(solution)/shard_map/stack | solution.py:303
  149.3 56.8 %scatter.1 = (bf16[128,512]{1,0:T(8,128)(2,1)S(1)}, bf16[128,512]{1,0:T(8,128)(2,1)S(1)}) custom-call(bf16[1024,2048]{1,0:T(8,128)(2,1)S(1)} %add_convert_fusion.1.m_ref, bf16[1024,2048]{1,0:T(8,128)(2,1)S(1)} %add_convert_fusion.g_ref), custom_call_target="tpu_custom_call" | custom-call | tf_op jit(solution)/shard_map/scatter/pallas_call | solution.py:243
  206.2 0.0 all-to-all-done
  206.2 0.0 copy-done.10
  206.2 0.6 select_reduce_fusion
  206.8 0.7 copy.32
  207.5 0.7 copy.33
  (7 shorter events, 0.0 us)
Async XLA Ops:
  56.7 4.9 %copy-start.3 = (bf16[2,2048,256]{2,1,0:T(8,128)(2,1)S(1)}, bf16[2,2048,256]{2,1,0:T(8,128)(2,1)}, u32[]{:S(2)}) copy-start(bf16[2,2048,256]{2,1,0:T(8,128)(2,1)} %param.12) | copy-start | bytes 6291460
  56.7 4.9 %copy-start.13 = (bf16[1024,2048]{1,0:T(8,128)(2,1)S(1)}, bf16[1024,2048]{1,0:T(8,128)(2,1)}, u32[]{:S(2)}) copy-start(bf16[1024,2048]{1,0:T(8,128)(2,1)} %get-tuple-element.11) | copy-start | bytes 12582916
  61.7 2.3 %copy-start = (bf16[2,2048,256]{2,1,0:T(8,128)(2,1)S(1)}, bf16[2,2048,256]{2,1,0:T(8,128)(2,1)}, u32[]{:S(2)}) copy-start(bf16[2,2048,256]{2,1,0:T(8,128)(2,1)} %param.11) | copy-start | bytes 6291460
  66.2 2.3 %copy-start.9 = (bf16[1024,128]{1,0:T(8,128)(2,1)S(1)}, bf16[1024,128]{1,0:T(8,128)(2,1)}, u32[]{:S(2)}) copy-start(bf16[1024,128]{1,0:T(8,128)(2,1)} %get-tuple-element.12) | copy-start | bytes 786436
  69.1 6.0 %copy-start.1 = (bf16[2,256,2048]{2,1,0:T(8,128)(2,1)S(1)}, bf16[2,256,2048]{2,1,0:T(8,128)(2,1)}, u32[]{:S(2)}) copy-start(bf16[2,256,2048]{2,1,0:T(8,128)(2,1)} %param.13) | copy-start | bytes 6291460
  69.1 6.0 %copy-start.11 = (bf16[1024,2048]{1,0:T(8,128)(2,1)S(1)}, bf16[1024,2048]{1,0:T(8,128)(2,1)}, u32[]{:S(2)}) copy-start(bf16[1024,2048]{1,0:T(8,128)(2,1)} %get-tuple-element.13) | copy-start | bytes 12582916
  69.1 6.0 %copy-start.15 = (f32[1024,256]{0,1:T(8,128)S(1)}, f32[1024,256]{0,1:T(8,128)}, u32[]{:S(2)}) copy-start(f32[1024,256]{0,1:T(8,128)} %fusion.16) | copy-start | bytes 3145732
  69.1 6.0 %copy-start.16 = (f32[1024,256]{0,1:T(8,128)S(1)}, f32[1024,256]{0,1:T(8,128)}, u32[]{:S(2)}) copy-start(f32[1024,256]{0,1:T(8,128)} %fusion.20) | copy-start | bytes 3145732
  86.5 119.7 %all-to-all-start = ((f32[8,128,2]{1,2,0:T(2,128)}), f32[8,128,2]{1,2,0:T(2,128)S(1)}, u32[]{:S(2)}, u32[]{:S(2)}) async-start(f32[8,128,2]{1,2,0:T(2,128)} %copy.26), calls=%async_computation | async-start | bytes 16384 | tf_op jit(solution)/shard_map/all_to_all | solution.py:307
  102.3 4.5 %copy-start.6 = (bf16[1024,256]{0,1:T(8,128)(2,1)S(1)}, bf16[1024,256]{0,1:T(8,128)(2,1)}, u32[]{:S(2)}) copy-start(bf16[1024,256]{0,1:T(8,128)(2,1)} %get-tuple-element.25) | copy-start | bytes 1572868
  102.3 4.5 %copy-start.14 = (bf16[1024,2048]{1,0:T(8,128)(2,1)S(1)}, bf16[1024,2048]{1,0:T(8,128)(2,1)}, u32[]{:S(2)}) copy-start(bf16[1024,2048]{1,0:T(8,128)(2,1)} %get-tuple-element.11) | copy-start | bytes 12582916
  106.8 2.7 %copy-start.4 = (bf16[2,2048,256]{2,1,0:T(8,128)(2,1)S(1)}, bf16[2,2048,256]{2,1,0:T(8,128)(2,1)}, u32[]{:S(2)}) copy-start(bf16[2,2048,256]{2,1,0:T(8,128)(2,1)} %param.12) | copy-start | bytes 6291460
  109.5 4.5 %copy-start.5 = (bf16[1024,256]{0,1:T(8,128)(2,1)S(1)}, bf16[1024,256]{0,1:T(8,128)(2,1)}, u32[]{:S(2)}) copy-start(bf16[1024,256]{0,1:T(8,128)(2,1)} %get-tuple-element.19) | copy-start | bytes 1572868
  116.8 4.5 %copy-start.12 = (bf16[1024,2048]{1,0:T(8,128)(2,1)S(1)}, bf16[1024,2048]{1,0:T(8,128)(2,1)}, u32[]{:S(2)}) copy-start(bf16[1024,2048]{1,0:T(8,128)(2,1)} %get-tuple-element.13) | copy-start | bytes 12582916
  121.3 1.6 copy-start.2
  122.9 1.3 copy-start.7
  124.2 2.8 %copy-start.8 = (bf16[1024,256]{0,1:T(8,128)(2,1)S(1)}, bf16[1024,256]{0,1:T(8,128)(2,1)}, u32[]{:S(2)}) copy-start(bf16[1024,256]{0,1:T(8,128)(2,1)} %get-tuple-element.22) | copy-start | bytes 1572868
  149.3 56.9 %copy-start.10 = (s32[128,8]{0,1:T(8,128)S(1)}, s32[128,8]{0,1:T(8,128)}, u32[]{:S(2)}) copy-start(s32[128,8]{0,1:T(8,128)} %param.9) | copy-start | bytes 12292

commit v3 on v2

--- a/solution.py
+++ b/solution.py
@@ -269,6 +269,43 @@
     return lax.dot_general(a, b, (((ca,), (cb,)), ((), ())), preferred_element_type=F32)
 
 
+def grads_kernel(mine, x_ref, c_ref, *refs):
+    gate_out, up_out, down_out = refs[3 * mine :]
+    x, c = x_ref[...], c_ref[...]
+    for e in range(mine):
+        hidden, gate, up = (ref[...] for ref in refs[3 * e : 3 * e + 3])
+        gate_out[e] = dot(x, gate, 0, 0)
+        up_out[e] = dot(x, up, 0, 0)
+        down_out[e] = dot(hidden, c, 0, 0)
+
+
+def weight_grads(x, c, weighted, pre_grads):
+    mine, (total, features), units = len(weighted), x.shape, weighted[0].shape[1]
+    width = 512
+    columns = pl.BlockSpec((total, width), lambda j: (0, j))
+    tall = pl.BlockSpec((mine, width, units), lambda j: (0, j, 0))
+    flat = [a for e in range(mine) for a in (weighted[e], pre_grads[2 * e], pre_grads[2 * e + 1])]
+    return pl.pallas_call(
+        functools.partial(grads_kernel, mine),
+        grid=(features // width,),
+        out_shape=(
+            jax.ShapeDtypeStruct((mine, features, units), F32),
+            jax.ShapeDtypeStruct((mine, features, units), F32),
+            jax.ShapeDtypeStruct((mine, units, features), F32),
+        ),
+        in_specs=[columns, columns]
+        + [pl.BlockSpec((total, units), lambda j: (0, 0)) for _ in flat],
+        out_specs=[tall, tall, pl.BlockSpec((mine, units, width), lambda j: (0, 0, j))],
+        compiler_params=pltpu.CompilerParams(vmem_limit_bytes=40 * 2**20),
+        cost_estimate=pl.CostEstimate(
+            flops=6 * mine * total * features * units,
+            bytes_accessed=4 * total * features + 12 * mine * features * units,
+            transcendentals=0,
+        ),
+        name="weight_grads",
+    )(x, c, *flat)
+
+
 def piece(tokens, cotangent, expert_ids, route_gates, gate_proj, up_proj, down_proj):
     groups = lax.axis_size("dp")
     mine, features, units = gate_proj.shape
@@ -300,9 +337,9 @@
         for e in range(mine)
     ).astype(BF16)
     sums = lax.optimization_barrier(scatter(out_part, in_part))
-    grad_down = jnp.stack([dot(weighted[e], c, 0, 0) for e in range(mine)])
-    grad_gate_w = jnp.stack([dot(x, pre_grads[2 * e], 0, 0) for e in range(mine)])
-    grad_up_w = jnp.stack([dot(x, pre_grads[2 * e + 1], 0, 0) for e in range(mine)])
+    grad_gate_w, grad_up_w, grad_down = lax.optimization_barrier(
+        weight_grads(x, c, weighted, pre_grads)
+    )
     inner = lax.psum(jnp.stack(inner, 1), "et").reshape(groups, rows, mine)
     inner = lax.all_to_all(inner, "dp", 0, 0, tiled=True).transpose(1, 0, 2).reshape(rows, experts)
     grad_gates = jnp.sum(jnp.where(chosen, inner[:, None, :], 0.0), axis=2)

time: 209 us -> 199 us (0.952)
  matrix products: 62.3 us -> 51.1 us
  Pallas kernels: 111 us -> 121 us
  other arithmetic: 11.8 us -> 2.29 us
    dot_general x18 -> x12, matrix products: 62.3 us -> 51.1 us  [dot(): lax.dot_general(a, b, (((ca,), (cb,)), ((), ())), preferred_element_type=...]
    pallas_call x0 -> x1, Pallas kernels: none -> 9.71 us  [weight_grads(): pl.pallas_call(functools.partial(grads_kernel, mine), grid=(features // w...]
    another operation x2 -> x0, other arithmetic: 9.68 us -> none  [the longest x1 7.4 us: piece(): jnp.stack([dot(x, pre_grads[2 * e], 0, 0) for e in range(mine)])]
  transfers between devices with their start and end apart: 1 -> 1, of which waited for: 0 -> 0; matrix products, arithmetic and copies ran while one was open for 25% -> 17% of each run, Pallas kernels for 27% -> 34%
where the time goes in v3:
time: 199 us; the launch traced here: 198 us
  Pallas kernels  121 us (61%)
  matrix products  51.1 us (26%)
  starting transfers between devices  11 us (6%)
  blocking collectives  7.81 us (4%)
  local copies, waits for them, and re-layouts  4.62 us (2%)
  other arithmetic  2.29 us (1%)
    pallas_call x1, Pallas kernels, scatter(): pl.pallas_call(functools.partial(scatter_kernel, size), out_shape=(one, o...  56.9 us
    pallas_call x1, Pallas kernels, gather(): pl.pallas_call(functools.partial(gather_kernel, size), out_shape=(whole,...  53.9 us
    dot_general x12, matrix products, dot(): lax.dot_general(a, b, (((ca,), (cb,)), ((), ())), preferred_element_type=...  51.1 us
    all_to_all x1, starting transfers between devices, piece(): lax.all_to_all(inner, 'dp', 0, 0, tiled=True).transpose(1, 0, 2)  11 us
    pallas_call x1, Pallas kernels, weight_grads(): pl.pallas_call(functools.partial(grads_kernel, mine), grid=(features // w...  9.71 us
    psum x1, blocking collectives, piece(): inner = lax.psum(jnp.stack(inner, 1), 'et').reshape(groups, rows, mine)  7.81 us
  transfers between devices with their start and end apart: 1, of which 0 were waited for; matrix products, arithmetic and copies ran while one was open for 17% of the time, Pallas kernels for 34%

profile of v3, /device:TPU:0, one launch (start us, length us, event | category | flops | bytes accessed | tf_op | source)
XLA Modules:
  0.0 198.2 jit_solution(7640808277735291767)
XLA Ops:
  0.6 0.0 copy-start.8
  0.6 0.8 convert_element_type.33
  1.5 0.7 select_reduce_fusion.1
  2.2 0.1 copy.81
  2.3 0.6 pad.5.w_ref
  2.9 53.9 %gather.1 = (bf16[1024,2048]{1,0:T(8,128)(2,1)}, bf16[1024,2048]{1,0:T(8,128)(2,1)}, bf16[1024,128]{1,0:T(8,128)(2,1)}) custom-call(bf16[128,512]{1,0:T(8,128)(2,1)} %t_ref.1, bf16[128,512]{1,0:T(8,128)(2,1)} %c_ref.1, bf16[128,128]{1,0:T(8,128)(2,1)} %pad.5.w_ref), custom_call_target="tpu_custom_call" | custom-call | tf_op jit(solution)/shard_map/gather/pallas_call | solution.py:133
  56.9 0.0 copy-start
  56.9 3.9 %fusion.4 = f32[1024,256]{1,0:T(8,128)S(1)} fusion(bf16[1024,2048]{1,0:T(8,128)(2,1)} %get-tuple-element.14.x_ref, bf16[2,2048,256]{2,1,0:T(8,128)(2,1)} %param.12), kind=kOutput, calls=%fused_computation.6 | convolution fusion | flops 1073741824 | bytes 6291456 | tf_op jit(solution)/shard_map/dot_general | solution.py:269
  60.8 0.0 copy-done.8
  60.8 0.0 copy-done
  60.8 0.0 copy-start.4
  60.8 2.2 %fusion.16 = f32[1024,256]{1,0:T(8,128)} fusion(bf16[1024,2048]{1,0:T(8,128)(2,1)S(1)} %copy-done, bf16[2,2048,256]{2,1,0:T(8,128)(2,1)S(1)} %copy-done.8), kind=kOutput, calls=%fused_computation.18 | convolution fusion | flops 1073741824 | bytes 6291456 | tf_op jit(solution)/shard_map/dot_general | solution.py:269
  63.1 0.0 copy-done.4
  63.1 2.2 %fusion.8 = f32[1024,256]{1,0:T(8,128)} fusion(bf16[1024,2048]{1,0:T(8,128)(2,1)S(1)} %copy-done, bf16[2,2048,256]{2,1,0:T(8,128)(2,1)S(1)} %copy-done.4), kind=kOutput, calls=%fused_computation.10 | convolution fusion | flops 1073741824 | bytes 6291456 | tf_op jit(solution)/shard_map/dot_general | solution.py:269
  65.3 0.0 copy-start.10
  65.3 2.2 %fusion.20 = f32[1024,256]{1,0:T(8,128)} fusion(bf16[1024,2048]{1,0:T(8,128)(2,1)S(1)} %copy-done, bf16[2,2048,256]{2,1,0:T(8,128)(2,1)S(1)} %copy-done.4), kind=kOutput, calls=%fused_computation.22 | convolution fusion | flops 1073741824 | bytes 6291456 | tf_op jit(solution)/shard_map/dot_general | solution.py:269
  67.5 0.0 copy-done.10
  67.5 0.1 dynamic-slice_convert_fusion
  67.7 0.5 slice_reduce_fusion
  68.2 0.0 copy-start.2
  68.2 0.0 copy-start.6
  68.2 0.0 copy-start.12
  68.2 0.0 copy-start.13
  68.2 4.7 %multiply_reduce_fusion = (f32[1024]{0:T(1024)S(1)}, bf16[1024,256]{1,0:T(8,128)(2,1)S(1)}, bf16[1024,256]{1,0:T(8,128)(2,1)S(1)}, bf16[1024,256]{1,0:T(8,128)(2,1)S(1)}) fusion(f32[1024,256]{1,0:T(8,128)S(1)} %fusion.4, f32[1024,256]{1,0:T(8,128)} %fusion.8, f32[1024]{0:T(1024)S(1)} %get-tuple-element.22, bf16[1024,2048]{1,0:T(8,128)(2,1)} %get-tuple-element.16.c_ref, ...), kind=kOutput, calls=%fused_computation.24 | convolution fusion | flops 1078721536 | bytes 8921088 | tf_op jit(solution)/shard_map/dot_general | solution.py:269
  72.9 0.0 copy-done.2
  72.9 0.0 copy-done.6
  72.9 0.2 copy-done.12
  73.1 0.3 copy-done.13
  73.4 1.8 multiply_reduce_fusion.1
  75.3 7.8 %psum.7 = f32[8,128,2]{1,0,2:T(8,128)S(1)} all-reduce(f32[8,128,2]{1,0,2:T(8,128)S(1)} %bitcast.59), channel_id=1, replica_groups=mesh['dp'=8,'et'=4] {'et'}, use_global_device_ids=true, to_apply=%region_3.4 | all-reduce | flops 2048 | bytes 16384 | tf_op jit(solution)/shard_map/psum | solution.py:343
  83.1 0.6 copy.96
  83.7 11.0 %all-to-all-start = ((f32[8,128,2]{1,2,0:T(2,128)}), f32[8,128,2]{1,2,0:T(2,128)S(1)}, u32[]{:S(2)}, u32[]{:S(2)}) async-start(f32[8,128,2]{1,2,0:T(2,128)} %copy.96), calls=%async_computation | async-start | bytes 16384 | tf_op jit(solution)/shard_map/all_to_all | solution.py:344
  94.7 0.0 copy-start.9
  94.7 5.9 %fusion.6 = f32[1024,2048]{1,0:T(8,128)} fusion(bf16[1024,256]{1,0:T(8,128)(2,1)S(1)} %get-tuple-element.27.refs_4_, bf16[2,2048,256]{2,1,0:T(8,128)(2,1)} %param.11), kind=kOutput, calls=%fused_computation.8 | convolution fusion | flops 1073741824 | bytes 9961472 | tf_op jit(solution)/shard_map/dot_general | solution.py:269
  100.6 0.0 copy-done.9
  100.6 0.0 copy-start.5
  100.6 4.5 %fusion.14 = f32[1024,2048]{1,0:T(8,128)} fusion(bf16[1024,256]{1,0:T(8,128)(2,1)S(1)} %get-tuple-element.31.refs_2_, bf16[2,2048,256]{2,1,0:T(8,128)(2,1)S(1)} %copy-done.9), kind=kOutput, calls=%fused_computation.16 | convolution fusion | flops 1073741824 | bytes 9961472 | tf_op jit(solution)/shard_map/dot_general | solution.py:269
  105.1 0.0 copy-done.5
  105.1 0.0 copy-start.7
  105.1 4.5 %fusion.18 = f32[1024,2048]{1,0:T(8,128)} fusion(bf16[1024,256]{1,0:T(8,128)(2,1)S(1)} %get-tuple-element.25.refs_1_, bf16[2,2048,256]{2,1,0:T(8,128)(2,1)S(1)} %copy-done.5), kind=kOutput, calls=%fused_computation.20 | convolution fusion | flops 1073741824 | bytes 9961472 | tf_op jit(solution)/shard_map/dot_general | solution.py:269
  109.6 0.0 copy-done.7
  109.6 0.0 copy-start.1
  109.6 0.0 copy-start.3
  109.6 5.5 %fusion.12 = f32[1024,2048]{1,0:T(8,128)} fusion(bf16[1024,256]{1,0:T(8,128)(2,1)S(1)} %get-tuple-element.30.refs_0_, bf16[2,256,2048]{2,1,0:T(8,128)(2,1)S(1)} %copy-done.7), kind=kOutput, calls=%fused_computation.14 | convolution fusion | flops 1073741824 | bytes 9961472 | tf_op jit(solution)/shard_map/dot_general | solution.py:269
  115.0 0.0 copy-done.1
  115.0 0.9 copy-done.3
  116.0 9.7 %weight_grads.1 = (f32[2,2048,256]{2,1,0:T(8,128)}, f32[2,2048,256]{2,1,0:T(8,128)}, f32[2,256,2048]{2,1,0:T(8,128)}) custom-call(bf16[1024,2048]{1,0:T(8,128)(2,1)S(1)} %copy-done.1, bf16[1024,2048]{1,0:T(8,128)(2,1)S(1)} %copy-done.3, bf16[1024,256]{1,0:T(8,128)(2,1)S(1)} %get-tuple-element.30.refs_0_, bf16[1024,256]{1,0:T(8,128)(2,1)S(1)} %get-tuple-element.25.refs_1_, ...), custom_call_target="tpu_custom_call" | custom-call | flops 6442450944 | bytes 20971520 | tf_op jit(solution)/shard_map/weight_grads/pallas_call | solution.py:288
  125.7 9.0 %add_convert_fusion.g_ref = bf16[1024,2048]{1,0:T(8,128)(2,1)S(1)} fusion(f32[1024,2048]{1,0:T(8,128)} %fusion.6, f32[1024,2048]{1,0:T(8,128)} %fusion.18, f32[1024,2048]{1,0:T(8,128)} %fusion.14, bf16[1024,256]{1,0:T(8,128)(2,1)S(1)} %get-tuple-element.29.refs_5_, bf16[2,2048,256]{2,1,0:T(8,128)(2,1)S(1)} %copy-done.9), kind=kOutput, calls=%fused_computation | convolution fusion | flops 1082130432 | bytes 30932992 | tf_op jit(solution)/shard_map/dot_general | solution.py:269
  134.7 4.6 %add_convert_fusion.1.m_ref = bf16[1024,2048]{1,0:T(8,128)(2,1)S(1)} fusion(f32[1024,2048]{1,0:T(8,128)} %fusion.12, bf16[1024,256]{1,0:T(8,128)(2,1)S(1)} %get-tuple-element.28.refs_3_, bf16[2,256,2048]{2,1,0:T(8,128)(2,1)S(1)} %copy-done.7), kind=kOutput, calls=%fused_computation.1 | convolution fusion | flops 1077936128 | bytes 14155776 | tf_op jit(solution)/shard_map/dot_general | solution.py:269
  139.4 0.0 copy-start.11
  139.4 56.9 %scatter.1 = (bf16[128,512]{1,0:T(8,128)(2,1)S(1)}, bf16[128,512]{1,0:T(8,128)(2,1)S(1)}) custom-call(bf16[1024,2048]{1,0:T(8,128)(2,1)S(1)} %add_convert_fusion.1.m_ref, bf16[1024,2048]{1,0:T(8,128)(2,1)S(1)} %add_convert_fusion.g_ref), custom_call_target="tpu_custom_call" | custom-call | tf_op jit(solution)/shard_map/scatter/pallas_call | solution.py:243
  196.3 0.0 all-to-all-done
  196.3 0.0 copy-done.11
  196.3 0.6 select_reduce_fusion
  196.9 0.7 copy.108
  197.6 0.7 copy.109
  (2 shorter events, 0.0 us)
Async XLA Ops:
  0.6 60.2 %copy-start.8 = (bf16[2,2048,256]{2,1,0:T(8,128)(2,1)S(1)}, bf16[2,2048,256]{2,1,0:T(8,128)(2,1)}, u32[]{:S(2)}) copy-start(bf16[2,2048,256]{2,1,0:T(8,128)(2,1)} %param.12) | copy-start | bytes 6291460
  56.9 3.9 %copy-start = (bf16[1024,2048]{1,0:T(8,128)(2,1)S(1)}, bf16[1024,2048]{1,0:T(8,128)(2,1)}, u32[]{:S(2)}) copy-start(bf16[1024,2048]{1,0:T(8,128)(2,1)} %get-tuple-element.14.x_ref) | copy-start | bytes 12582916
  60.8 2.3 %copy-start.4 = (bf16[2,2048,256]{2,1,0:T(8,128)(2,1)S(1)}, bf16[2,2048,256]{2,1,0:T(8,128)(2,1)}, u32[]{:S(2)}) copy-start(bf16[2,2048,256]{2,1,0:T(8,128)(2,1)} %param.11) | copy-start | bytes 6291460
  65.3 2.2 %copy-start.10 = (bf16[1024,128]{1,0:T(8,128)(2,1)S(1)}, bf16[1024,128]{1,0:T(8,128)(2,1)}, u32[]{:S(2)}) copy-start(bf16[1024,128]{1,0:T(8,128)(2,1)} %get-tuple-element.15) | copy-start | bytes 786436
  68.2 4.8 %copy-start.2 = (bf16[1024,2048]{1,0:T(8,128)(2,1)S(1)}, bf16[1024,2048]{1,0:T(8,128)(2,1)}, u32[]{:S(2)}) copy-start(bf16[1024,2048]{1,0:T(8,128)(2,1)} %get-tuple-element.16.c_ref) | copy-start | bytes 12582916
  68.2 4.8 %copy-start.6 = (bf16[2,256,2048]{2,1,0:T(8,128)(2,1)S(1)}, bf16[2,256,2048]{2,1,0:T(8,128)(2,1)}, u32[]{:S(2)}) copy-start(bf16[2,256,2048]{2,1,0:T(8,128)(2,1)} %param.13) | copy-start | bytes 6291460
  68.2 4.9 %copy-start.12 = (f32[1024,256]{1,0:T(8,128)S(1)}, f32[1024,256]{1,0:T(8,128)}, u32[]{:S(2)}) copy-start(f32[1024,256]{1,0:T(8,128)} %fusion.16) | copy-start | bytes 3145732
  68.2 5.2 %copy-start.13 = (f32[1024,256]{1,0:T(8,128)S(1)}, f32[1024,256]{1,0:T(8,128)}, u32[]{:S(2)}) copy-start(f32[1024,256]{1,0:T(8,128)} %fusion.20) | copy-start | bytes 3145732
  83.7 112.6 %all-to-all-start = ((f32[8,128,2]{1,2,0:T(2,128)}), f32[8,128,2]{1,2,0:T(2,128)S(1)}, u32[]{:S(2)}, u32[]{:S(2)}) async-start(f32[8,128,2]{1,2,0:T(2,128)} %copy.96), calls=%async_computation | async-start | bytes 16384 | tf_op jit(solution)/shard_map/all_to_all | solution.py:344
  94.7 5.9 %copy-start.9 = (bf16[2,2048,256]{2,1,0:T(8,128)(2,1)S(1)}, bf16[2,2048,256]{2,1,0:T(8,128)(2,1)}, u32[]{:S(2)}) copy-start(bf16[2,2048,256]{2,1,0:T(8,128)(2,1)} %param.12) | copy-start | bytes 6291460
  100.6 4.5 %copy-start.5 = (bf16[2,2048,256]{2,1,0:T(8,128)(2,1)S(1)}, bf16[2,2048,256]{2,1,0:T(8,128)(2,1)}, u32[]{:S(2)}) copy-start(bf16[2,2048,256]{2,1,0:T(8,128)(2,1)} %param.11) | copy-start | bytes 6291460
  105.1 4.5 %copy-start.7 = (bf16[2,256,2048]{2,1,0:T(8,128)(2,1)S(1)}, bf16[2,256,2048]{2,1,0:T(8,128)(2,1)}, u32[]{:S(2)}) copy-start(bf16[2,256,2048]{2,1,0:T(8,128)(2,1)} %param.13) | copy-start | bytes 6291460
  109.6 5.5 %copy-start.1 = (bf16[1024,2048]{1,0:T(8,128)(2,1)S(1)}, bf16[1024,2048]{1,0:T(8,128)(2,1)}, u32[]{:S(2)}) copy-start(bf16[1024,2048]{1,0:T(8,128)(2,1)} %get-tuple-element.14.x_ref) | copy-start | bytes 12582916
  109.6 6.4 %copy-start.3 = (bf16[1024,2048]{1,0:T(8,128)(2,1)S(1)}, bf16[1024,2048]{1,0:T(8,128)(2,1)}, u32[]{:S(2)}) copy-start(bf16[1024,2048]{1,0:T(8,128)(2,1)} %get-tuple-element.16.c_ref) | copy-start | bytes 12582916
  139.4 56.9 %copy-start.11 = (s32[128,8]{0,1:T(8,128)S(1)}, s32[128,8]{0,1:T(8,128)}, u32[]{:S(2)}) copy-start(s32[128,8]{0,1:T(8,128)} %param.9) | copy-start | bytes 12292
